TPU v7x, 256 devices: a whole 4x4x8 slice. The times are simulated.
256 devices in a mesh: dir: 2 (over z_lo), row: 8 (over z_hi, core), col: 16 (over y, x).
Axes of the slice: x: 4, y: 4, z: 8 (z_hi: 4, z_lo: 2; z = z_hi * 2 + z_lo), core: 2. Of those that a mesh axis runs over, the one named last changes fastest.
Arguments:
- prior_y: float32 [2, 12288, 12288], P('dir', 'row', 'col'), as said below
- labels: int32 [12288, 4], replicated, may hold values from 0 to 7
- pivots: int32 [2, 2], replicated, may hold values from 1 to 47, as said below
Outputs:
- schur: float32 [8, 2, 768, 12288], P('row', 'dir', None, 'col')
- lower: float32 [8, 2, 768, 256], P('row', 'dir')
Inputs may be any that keep to these rules, and one draw needn't show every extreme that they name: `prior_y`: each direction's matrix is symmetric and positive definite. `pivots`: the two tiles of a direction differ, tile 0 is never named, and all four entries differ.
All inputs are finite; a program needn't handle non-finite values.
Results may differ from a plain program's by a relative error of at most 0.00011.
Values sent between devices are 32-bit elements; how exact they have to be, the bound alone decides.
A program may use at most 128 MiB of HBM per device.

v0:
```python
import jax
import jax.numpy as jnp
from jax import lax
from jax.sharding import PartitionSpec as P

TILE = 256


def broadcast(block, axis, owner):
    block = jnp.where(lax.axis_index(axis) == owner, block, jnp.zeros_like(block))
    return lax.psum(block, axis)


def solve_parts(col_panel, row_panel, pivot):
    factor = jnp.linalg.cholesky(pivot)
    right = jax.scipy.linalg.cho_solve((factor, True), row_panel)
    left = jax.scipy.linalg.cho_solve((factor, True), col_panel.T).T
    inverse = jax.scipy.linalg.cho_solve((factor, True), jnp.eye(pivot.shape[0], dtype=jnp.float32))
    return (right, left, inverse)


def sweep_rows(block, row_first, col_first, col_panel, right, left, inverse, tile_index):
    updated = block - jnp.dot(col_panel, right, precision=lax.Precision.HIGHEST)
    start = tile_index * TILE
    row_ids = row_first + jnp.arange(block.shape[0], dtype=jnp.int32)
    col_ids = col_first + jnp.arange(block.shape[1], dtype=jnp.int32)
    row_hit = (row_ids // TILE == tile_index)[:, None]
    col_hit = (col_ids // TILE == tile_index)[None, :]
    col_start = jnp.clip(start - col_first, 0, block.shape[1] - TILE)
    row_start = jnp.clip(start - row_first, 0, block.shape[0] - TILE)
    zero = jnp.zeros((), jnp.int32)
    updated = jnp.where(
        col_hit, lax.dynamic_update_slice(updated, left, (zero, col_start)), updated
    )
    updated = jnp.where(
        row_hit, lax.dynamic_update_slice(updated, right, (row_start, zero)), updated
    )
    updated = jnp.where(
        row_hit & col_hit,
        lax.dynamic_update_slice(updated, -inverse, (row_start, col_start)),
        updated,
    )
    return updated


def col_slice(matrix, tile_index, col_first):
    start = jnp.clip(tile_index * TILE - col_first, 0, matrix.shape[1] - TILE)
    return lax.dynamic_slice_in_dim(matrix, start, TILE, 1)


def share_columns(local_cols, tile_index, width):
    return broadcast(local_cols, "col", tile_index * TILE // width)


def share_rows(matrix, col_panel, tile_index, row_first):
    height = matrix.shape[0]
    start = jnp.clip(tile_index * TILE - row_first, 0, height - TILE)
    packed = jnp.concatenate(
        [
            lax.dynamic_slice_in_dim(matrix, start, TILE, 0),
            lax.dynamic_slice_in_dim(col_panel, start, TILE, 0),
        ],
        axis=1,
    )
    return broadcast(packed, "row", tile_index * TILE // height)


def per_device(prior_y, labels, pivots):
    grid_row = lax.axis_index("row")
    grid_col = lax.axis_index("col")
    direction = lax.axis_index("dir")
    height = prior_y.shape[1]
    width = prior_y.shape[2]
    half = height // 2
    row_first = grid_row * height
    col_first = grid_col * width
    quantum = lax.dynamic_slice_in_dim(labels, row_first, height, 0).astype(jnp.float32)
    shift = (
        0.025 * quantum[:, 0] * (quantum[:, 0] + 1.0)
        + 0.01 * quantum[:, 1] * quantum[:, 1]
        + 0.01 * quantum[:, 2] * (quantum[:, 2] + 1.0)
        + 0.005 * quantum[:, 3] * (quantum[:, 3] + 1.0)
    )
    row_ids = row_first + jnp.arange(height, dtype=jnp.int32)
    col_ids = col_first + jnp.arange(width, dtype=jnp.int32)
    matrix = prior_y[0] + jnp.where(row_ids[:, None] == col_ids[None, :], shift[:, None], 0.0)
    first_tile = pivots[direction, 0]
    second_tile = pivots[direction, 1]
    col_panel = share_columns(col_slice(matrix, first_tile, col_first), first_tile, width)
    packed = share_rows(matrix, col_panel, first_tile, row_first)
    right, left, inverse = solve_parts(col_panel, packed[:, :width], packed[:, width:])
    swept = sweep_rows(matrix, row_first, col_first, col_panel, right, left, inverse, first_tile)
    next_panel = share_columns(col_slice(swept, second_tile, col_first), second_tile, width)
    next_packed = share_rows(swept, next_panel, second_tile, row_first)
    half_first = row_first + direction * half
    next_right, next_left, next_inverse = solve_parts(
        next_panel, next_packed[:, :width], next_packed[:, width:]
    )
    final = sweep_rows(
        swept, row_first, col_first, next_panel, next_right, next_left, next_inverse, second_tile
    )
    received = lax.all_to_all(final, "dir", split_axis=0, concat_axis=0, tiled=True)
    match = received[:half] + received[half:]
    match_panel = broadcast(match[:, :TILE], "col", 0)
    leading = broadcast(
        jnp.concatenate([match[:TILE, :], match_panel[:TILE, :]], axis=1), ("dir", "row"), 0
    )
    factor = jnp.linalg.cholesky(leading[:, width:])
    lower = jax.scipy.linalg.cho_solve((factor, True), match_panel.T).T
    schur = match - jnp.dot(lower, leading[:, :width], precision=lax.Precision.HIGHEST)
    half_ids = half_first + jnp.arange(half, dtype=jnp.int32)
    keep = (half_ids < TILE)[:, None] | (col_ids < TILE)[None, :]
    schur = jnp.where(keep, match, schur)
    return (schur.reshape(1, 1, half, width), lower.reshape(1, 1, half, TILE))


def solution(mesh):
    placed = (P("dir", "row", "col"), P(), P())
    return jax.shard_map(
        per_device,
        mesh=mesh,
        in_specs=placed,
        out_specs=(P("row", "dir", None, "col"), P("row", "dir", None, None)),
        check_vma=False,
    )
```

profile of v0, /device:TPU:74, one launch (start us, length us, event | category | flops | bytes accessed | tf_op | source)
XLA Modules:
  0.0 953.5 jit_solution(16734866693029957239)
XLA Ops:
  9.3 6.1 copy.23
  24.1 98.0 %all-reduce.8.cloned.1.call-done = f32[1536,256]{0,1:T(8,128)} async-done(((f32[1536,256]{0,1:T(8,128)}), f32[1536,256]{0,1:T(8,128)}) %all-reduce.8.cloned.1.call-update) | async-done | bytes 1572880 | tf_op jit(solution)/shard_map/psum | solution.py:11
  130.2 70.0 %all-reduce.10.cloned.1.call-done = f32[256,1024]{0,1:T(8,128)} async-done(((f32[256,1024]{0,1:T(8,128)}), f32[256,1024]{0,1:T(8,128)}) %all-reduce.10.cloned.1.call-update) | async-done | bytes 1048592 | tf_op jit(solution)/shard_map/psum | solution.py:11
  202.5 11.7 %cholesky.172 = f32[128,128]{1,0:T(8,128)S(1)} custom-call(f32[128,128]{1,0:T(8,128)S(1)} %cholesky.270), custom_call_target="Cholesky" | custom-call | tf_op jit(solution)/shard_map/jit(cholesky)/cholesky | solution.py:15
  214.3 9.8 %custom-call.29 = f32[1,128,128]{1,2,0:T(8,128)S(1)} custom-call(f32[1,128,128]{2,1,0:T(8,128)S(1)} %get-tuple-element.110), custom_call_target="InvertDiagBlocksLowerTriangular" | custom-call | tf_op jit(solution)/shard_map/jit(cholesky)/cholesky | solution.py:15
  224.6 11.7 %cholesky.189 = f32[128,128]{1,0:T(8,128)S(1)} custom-call(f32[128,128]{1,0:T(8,128)S(1)} %convolution_subtract_fusion.18), custom_call_target="Cholesky" | custom-call | tf_op jit(solution)/shard_map/jit(cholesky)/cholesky | solution.py:15
  238.4 4.3 while.14
  242.6 19.7 %custom-call.30 = f32[2,128,128]{1,2,0:T(8,128)S(1)} custom-call(f32[2,128,128]{2,1,0:T(8,128)S(1)} %get-tuple-element.54), custom_call_target="InvertDiagBlocksLowerTriangular" | custom-call | tf_op jit(solution)/shard_map/jit(_cho_solve)/triangular_solve | solution.py:16
  277.6 16.0 %convolution_subtract_fusion.1 = f32[1536,768]{0,1:T(8,128)S(1)} fusion(f32[1536,768]{0,1:T(8,128)S(1)} %bitcast.200, f32[1536,256]{0,1:T(8,128)S(1)} %copy-done.3, f32[128,768]{0,1:T(8,128)S(1)} %copy.26, f32[128,768]{0,1:T(8,128)S(1)} %fusion.41), kind=kOutput, calls=%fused_computation.9 | convolution fusion | flops 3625254912 | bytes 11796480 | tf_op jit(solution)/shard_map/dot_general | solution.py:23
  296.1 4.6 select_n.209
  302.2 4.0 select_n.215
  314.2 99.2 %all-reduce.12.cloned.1.call-done = f32[1536,256]{0,1:T(8,128)} async-done(((f32[1536,256]{0,1:T(8,128)}), f32[1536,256]{0,1:T(8,128)}) %all-reduce.12.cloned.1.call-update) | async-done | bytes 1572880 | tf_op jit(solution)/shard_map/psum | solution.py:11
  417.5 73.9 %all-reduce.14.cloned.1.call-done = f32[256,1024]{0,1:T(8,128)} async-done(((f32[256,1024]{0,1:T(8,128)}), f32[256,1024]{0,1:T(8,128)}) %all-reduce.14.cloned.1.call-update) | async-done | bytes 1048592 | tf_op jit(solution)/shard_map/psum | solution.py:11
  493.5 11.7 %cholesky.206 = f32[128,128]{1,0:T(8,128)S(1)} custom-call(f32[128,128]{1,0:T(8,128)S(1)} %cholesky.273), custom_call_target="Cholesky" | custom-call | tf_op jit(solution)/shard_map/jit(cholesky)/cholesky | solution.py:15
  505.3 9.8 %custom-call.33 = f32[1,128,128]{1,2,0:T(8,128)S(1)} custom-call(f32[1,128,128]{2,1,0:T(8,128)S(1)} %get-tuple-element.106), custom_call_target="InvertDiagBlocksLowerTriangular" | custom-call | tf_op jit(solution)/shard_map/jit(cholesky)/cholesky | solution.py:15
  515.6 11.7 %cholesky.223 = f32[128,128]{1,0:T(8,128)S(1)} custom-call(f32[128,128]{1,0:T(8,128)S(1)} %convolution_subtract_fusion.17), custom_call_target="Cholesky" | custom-call | tf_op jit(solution)/shard_map/jit(cholesky)/cholesky | solution.py:15
  530.0 3.9 while.15
  533.9 20.1 %custom-call.34 = f32[2,128,128]{1,2,0:T(8,128)S(1)} custom-call(f32[2,128,128]{2,1,0:T(8,128)S(1)} %get-tuple-element.57), custom_call_target="InvertDiagBlocksLowerTriangular" | custom-call | tf_op jit(solution)/shard_map/jit(_cho_solve)/triangular_solve | solution.py:16
  568.0 4.6 convolution_subtract_fusion
  574.9 4.8 select_n.232
  581.3 4.7 select_n.237
  591.1 4.9 copy.50
  596.0 5.8 all-to-all-start
  601.8 52.4 %all-to-all-done = f32[2,768,768]{1,2,0:T(8,128)} async-done(((f32[2,768,768]{1,2,0:T(8,128)}), f32[2,768,768]{1,2,0:T(8,128)}, u32[]{:S(2)}, u32[]{:S(2)}) %all-to-all-start) | async-done | bytes 4718624 | tf_op jit(solution)/shard_map/all_to_all | solution.py:102
  660.6 92.8 %all-reduce.16.cloned.1.call-done = f32[768,256]{0,1:T(8,128)} async-done(((f32[768,256]{0,1:T(8,128)}), f32[768,256]{0,1:T(8,128)}) %all-reduce.16.cloned.1.call-update) | async-done | bytes 786448 | tf_op jit(solution)/shard_map/psum | solution.py:11
  755.6 111.0 %all-reduce.18.cloned.1.call-done = f32[256,1024]{0,1:T(8,128)} async-done(((f32[256,1024]{0,1:T(8,128)}), f32[256,1024]{0,1:T(8,128)}) %all-reduce.18.cloned.1.call-update) | async-done | bytes 1048592 | tf_op jit(solution)/shard_map/psum | solution.py:11
  871.1 11.7 %cholesky.240 = f32[128,128]{1,0:T(8,128)S(1)} custom-call(f32[128,128]{1,0:T(8,128)S(1)} %cholesky.276), custom_call_target="Cholesky" | custom-call | tf_op jit(solution)/shard_map/jit(cholesky)/cholesky | solution.py:108
  882.8 9.8 %custom-call.37 = f32[1,128,128]{1,2,0:T(8,128)S(1)} custom-call(f32[1,128,128]{2,1,0:T(8,128)S(1)} %get-tuple-element.102), custom_call_target="InvertDiagBlocksLowerTriangular" | custom-call | tf_op jit(solution)/shard_map/jit(cholesky)/cholesky | solution.py:108
  894.8 11.7 %cholesky.257 = f32[128,128]{1,0:T(8,128)S(1)} custom-call(f32[128,128]{1,0:T(8,128)S(1)} %convolution_subtract_fusion.16), custom_call_target="Cholesky" | custom-call | tf_op jit(solution)/shard_map/jit(cholesky)/cholesky | solution.py:108
  910.1 4.2 while.16
  914.9 20.5 %custom-call.38 = f32[2,128,128]{1,2,0:T(8,128)S(1)} custom-call(f32[2,128,128]{2,1,0:T(8,128)} %copy-done.15), custom_call_target="InvertDiagBlocksLowerTriangular" | custom-call | tf_op jit(solution)/shard_map/jit(_cho_solve)/triangular_solve | solution.py:109
  938.5 3.7 fusion
  (216 shorter events, 115.8 us)
Async XLA Ops:
  7.2 114.9 %all-reduce.8.cloned.1.call-start = ((), (), s32[]{:S(2)}) async-start(), calls=%async_computation.1 | async-start | bytes 3145728 | tf_op jit(solution)/shard_map/psum | solution.py:11
  19.0 2.1 copy-start.2
  22.6 177.7 %all-reduce.10.cloned.1.call-start = ((), (), s32[]{:S(2)}) async-start(), calls=%async_computation.2 | async-start | bytes 2097152 | tf_op jit(solution)/shard_map/psum | solution.py:11
  124.2 289.1 %all-reduce.12.cloned.1.call-start = ((), (), s32[]{:S(2)}) async-start(), calls=%async_computation.3 | async-start | bytes 3145728 | tf_op jit(solution)/shard_map/psum | solution.py:11
  200.3 62.1 %copy-start.7 = (f32[256,1024]{0,1:T(8,128)S(1)}, f32[256,1024]{0,1:T(8,128)}, u32[]{:S(2)}) copy-start(f32[256,1024]{0,1:T(8,128)} %all-reduce.10.cloned.1.call-done) | copy-start | bytes 3145732
  242.6 19.7 %copy-start.19 = (s32[2,2]{1,0:T(2,128)}, s32[2,2]{1,0:T(2,128)S(1)}, u32[]{:S(2)}) copy-start(s32[2,2]{1,0:T(2,128)S(1)} %get-tuple-element.282) | copy-start | bytes 52
  264.7 0.7 copy-start.5
  265.4 7.2 copy-start.3
  265.6 12.0 %slice-start.2 = ((s8[4718592]{0:T(1024)(128)(4,1)}), s8[524288]{0:T(1024)(128)(4,1)S(1)}, s32[]{:S(2)}) async-start(s8[4718592]{0:T(1024)(128)(4,1)} %bitcast.199), calls=%async_computation.9 | async-start | bytes 1048576
  273.5 4.1 slice-start.3
  293.7 2.1 copy-start
  300.7 5.5 copy-start.13
  300.7 5.9 copy-start.14
  300.7 5.9 copy-start.16
  300.7 5.9 copy-start.17
  312.5 178.8 %all-reduce.14.cloned.1.call-start = ((), (), s32[]{:S(2)}) async-start(), calls=%async_computation.4 | async-start | bytes 2097152 | tf_op jit(solution)/shard_map/psum | solution.py:11
  415.6 114.4 %copy-start.20 = (s32[2,2]{1,0:T(2,128)S(1)}, s32[2,2]{1,0:T(2,128)}, u32[]{:S(2)}) copy-start(s32[2,2]{1,0:T(2,128)} %copy-done.19) | copy-start | bytes 52
  491.3 62.7 %copy-start.8 = (f32[256,1024]{0,1:T(8,128)S(1)}, f32[256,1024]{0,1:T(8,128)}, u32[]{:S(2)}) copy-start(f32[256,1024]{0,1:T(8,128)} %all-reduce.14.cloned.1.call-done) | copy-start | bytes 3145732
  556.3 0.7 copy-start.6
  557.1 5.9 copy-start.4
  557.2 10.7 %slice-start = ((s8[4718592]{0:T(1024)(128)(4,1)}), s8[524288]{0:T(1024)(128)(4,1)S(1)}, s32[]{:S(2)}) async-start(s8[4718592]{0:T(1024)(128)(4,1)} %bitcast.196), calls=%async_computation.7 | async-start | bytes 1048576
  563.9 4.1 slice-start.1
  572.5 2.1 copy-start.1
  579.7 6.7 copy-start.18
  596.0 58.3 %all-to-all-start = ((f32[2,768,768]{1,2,0:T(8,128)}), f32[2,768,768]{1,2,0:T(8,128)}, u32[]{:S(2)}, u32[]{:S(2)}) async-start(f32[2,768,768]{1,2,0:T(8,128)} %bitcast.201), calls=%async_computation | async-start | bytes 9437184 | tf_op jit(solution)/shard_map/all_to_all | solution.py:102
  601.7 151.7 %all-reduce.16.cloned.1.call-start = ((), (), s32[]{:S(2)}) async-start(), calls=%async_computation.5 | async-start | bytes 1572864 | tf_op jit(solution)/shard_map/psum | solution.py:11
  657.9 208.7 %all-reduce.18.cloned.1.call-start = ((), (), s32[]{:S(2)}) async-start(), calls=%async_computation.6 | async-start | bytes 2097152 | tf_op jit(solution)/shard_map/psum | solution.py:11
  755.5 154.6 %copy-start.21 = (s32[2,2]{1,0:T(2,128)S(1)}, s32[2,2]{1,0:T(2,128)}, u32[]{:S(2)}) copy-start(s32[2,2]{1,0:T(2,128)} %copy-done.19) | copy-start | bytes 52
  755.5 179.9 %copy-start.10 = (f32[768,256]{0,1:T(8,128)S(1)}, f32[768,256]{0,1:T(8,128)}, u32[]{:S(2)}) copy-start(f32[768,256]{0,1:T(8,128)} %all-reduce.16.cloned.1.call-done) | copy-start | bytes 2359300
  870.3 0.7 copy-start.12
  907.2 1.8 copy-start.11
  937.0 1.6 copy-start.9
  (1 other events, 0.7 us)
Sparse Core Ops, SparseCore 0:
  22.7 99.3 all-reduce.7
  125.3 74.9 all-reduce.9
  312.6 100.6 all-reduce.11
  416.5 74.8 all-reduce.13
  658.0 95.4 all-reduce.15
  756.3 110.2 all-reduce.17
where the time goes:
time: 962 us; the launch traced here: 954 us
  waiting for transfers between devices  598 us (62%)
  other arithmetic  196 us (20%)
  local copies, waits for them, and re-layouts  75.7 us (8%)
  matrix products  57.4 us (6%)
  between operations  20.6 us (2%)
    psum x6, waiting for transfers between devices, broadcast(): return lax.psum(block, axis)  545 us
    another operation x13, other arithmetic, solve_parts(): factor = jnp.linalg.cholesky(pivot)  68.6 us
    all_to_all x1, waiting for transfers between devices, per_device(): lax.all_to_all(final, 'dir', split_axis=0, concat_axis=0, tiled=True)  52.4 us
    another operation x5, other arithmetic, solve_parts(): right = jax.scipy.linalg.cho_solve((factor, True), row_panel)  39.8 us
    another operation x7, other arithmetic, per_device(): factor = jnp.linalg.cholesky(leading[:, width:])  34.6 us
    another operation x2, other arithmetic, per_device(): lower = jax.scipy.linalg.cho_solve((factor, True), match_panel.T).T  21.5 us
    dot_general x2, matrix products, sweep_rows(): updated = block - jnp.dot(col_panel, right, precision=lax.Precision.HIGHEST)  20.6 us
    unnamed x55, local copies, waits for them, and re-layouts  19.5 us
  transfers between devices with their start and end apart: 7, of which 7 were waited for; matrix products, arithmetic and copies ran while one was open for 1% of the time, Pallas kernels for 0%

commit v1 on v0

v1 whole, which is shorter than its diff:
```python
import functools

import jax
import jax.numpy as jnp
from jax import lax
from jax.experimental import pallas as pl
from jax.experimental.pallas import tpu as pltpu
from jax.sharding import PartitionSpec as P

TILE = 256
F32 = jnp.float32
BF16 = jnp.bfloat16
MESH = pl.DeviceIdType.MESH
ROW_BY_COL = ((1,), (0,))
COL_BY_COL = ((0,), (0,))
TREE_ROWS = ((0, 48), (48, 48), (96, 80), (176, 80))
X_PARTS = 2


def dot6(a, b, dims):
    return lax.dot_general(
        a, b, (dims, ((), ())), precision=lax.Precision.HIGHEST, preferred_element_type=F32
    )


def split(x):
    high = x.astype(BF16)
    return high, (x - high.astype(F32)).astype(BF16)


def dot3(a, b, dims):
    ah, al = split(a)
    bh, bl = split(b)

    def one(p, q):
        return lax.dot_general(p, q, (dims, ((), ())), preferred_element_type=F32)

    return one(ah, bh) + (one(ah, bl) + one(al, bh))


def iota(shape, dim):
    return lax.broadcasted_iota(jnp.int32, shape, dim)


def sweep128(block, group=4):
    lanes, subs = iota((8, 128), 1), iota((8, 128), 0)
    width = 8 * group
    hits = [subs == k for k in range(8)]

    def body(_, b):
        s = [b[8 * j : 8 * j + 8, :] for j in range(group)]
        for i in range(group):
            v = [jnp.broadcast_to(s[i][:, 8 * i + m : 8 * i + m + 1], (8, 128)) for m in range(8)]
            for k in range(8):
                vk = v[k]
                inv = 1.0 / vk[k : k + 1, :]
                for j in range(8):
                    if j != k:
                        rj = v[j][k : k + 1, :] * inv
                        v[j] = jnp.where(hits[k], rj, v[j] - vk * rj)
                v[k] = jnp.where(hits[k], -inv, vk * inv)
            inside = (lanes >= 8 * i) & (lanes < 8 * i + 8)
            x = jnp.where(inside, jnp.where(lanes - 8 * i == subs, -1.0, 0.0), s[i])
            r = -v[0] * x[0:1, :]
            for m in range(1, 8):
                r = r - v[m] * x[m : m + 1, :]
            for q in range(1, group):
                j = (i + q) % group
                acc = jnp.where(inside, 0.0, s[j])
                for m in range(8):
                    col = jnp.broadcast_to(s[j][:, 8 * i + m : 8 * i + m + 1], (8, 128))
                    acc = acc - col * r[m : m + 1, :]
                s[j] = acc
            s[i] = r
        r = jnp.concatenate(s, axis=0)
        rest = b[width:, :]
        lane = iota(rest.shape, 1)
        rest = jnp.where(lane < width, 0.0, rest) - dot6(rest[:, :width], r, ROW_BY_COL)
        return pltpu.roll(jnp.concatenate([rest, r], axis=0), 128 - width, 1)

    return lax.fori_loop(0, 128 // width, body, block)


def sweep_step(a_ref, p):
    n = a_ref.shape[0]
    at = pl.multiple_of(p * 128, 128)
    neg = sweep128(a_ref[pl.ds(at, 128), pl.ds(at, 128)])
    x = a_ref[pl.ds(at, 128), :]
    col, row = iota((128, n), 1), iota((128, n), 0)
    x = jnp.where(col // 128 == p, jnp.where(col - at == row, -1.0, 0.0), x)
    r = -dot6(neg, x, ROW_BY_COL)
    a_ref[pl.ds(at, 128), :] = jnp.zeros((128, n), F32)
    a_ref[:, pl.ds(at, 128)] = jnp.zeros((n, 128), F32)
    a_ref[...] = a_ref[...] - dot6(x, r, COL_BY_COL)


def sweep_all(a_ref):
    def step(p, carry):
        sweep_step(a_ref, p)
        return carry

    lax.fori_loop(0, a_ref.shape[0] // 128, step, 0)


def modified(panel, tile, other, col_first):
    ids = col_first + iota(panel.shape, 1)
    local = ids - tile * TILE
    own = (local >= 0) & (local < TILE)
    beside = ids - other * TILE
    gone = (beside >= 0) & (beside < TILE)
    panel = jnp.where(own, jnp.where(local == iota(panel.shape, 0), -1.0, 0.0), panel)
    return jnp.where(gone, 0.0, panel)


def main_kernel(
    cand, pcand, prior, piv,
    raw, x_out, r_out, p0c_out, p0r_out, n_out,
    cm, pm, rs, y, hsib, p2, p2sum, p3, pv, g, u, mparts, pparts,
    sem_p1, sem_c1, s_p2, r_p2, s_p3, r_p3, s_p4, r_p4, s_p5, r_p5,
    s_rs, r_rs, s_h, r_h, s_agr, s_agl, r_ag,
    s_sib, r_sib, s_ga, s_gb, r_g, s_xa, s_xb, r_x, s_raw, r_raw, s_sw, r_sw,
):
    d, r, c = lax.axis_index("dir"), lax.axis_index("row"), lax.axis_index("col")
    s, z_hi = r % 2, r // 2
    z = 2 * z_hi + d
    cx, cy = c % 4, c // 4
    own = s == d

    def at(zz, cc):
        return (zz % 2, 2 * (zz // 2) + s, cc)

    sibling = (d, r + 1 - 2 * s, c)
    partner = (1 - d, r, c)

    def copy(src, dst, send, recv, device):
        return pltpu.make_async_remote_copy(
            src_ref=src, dst_ref=dst, send_sem=send, recv_sem=recv, device_id=device, device_id_type=MESH
        )

    barrier = pltpu.get_barrier_semaphore()
    pl.semaphore_signal(barrier, inc=1, device_id=sibling, device_id_type=MESH)
    for o in range(1, 8):
        pl.semaphore_signal(barrier, inc=1, device_id=at((z + o) % 8, c), device_id_type=MESH)
    for o in range(1, 16):
        pl.semaphore_signal(barrier, inc=1, device_id=at(z, (c + o) % 16), device_id_type=MESH)
    pl.semaphore_wait(barrier, 23)

    def merge_p():
        return copy(pcand, pm, sem_p1.at[0], sem_p1.at[1], sibling)

    def merge_c():
        return copy(cand, cm, sem_c1.at[0], sem_c1.at[1], sibling)

    def p2_copy(o, cc, slot):
        return copy(
            pm.at[pl.ds(pl.multiple_of(32 * cc, 32), 32), :], p2.at[slot], s_p2.at[o - 1], r_p2.at[slot], at(z, cc)
        )

    def rs_copy(o, q, slot):
        return copy(
            cm.at[pl.ds(0, 2), pl.ds(pl.multiple_of(64 * q, 64), 64), :],
            rs.at[slot], s_rs.at[o - 1], r_rs.at[slot], at(2 * q + d, c),
        )

    def h_copy(q):
        rows = pl.ds(pl.multiple_of(64 * q, 64), 64)
        return copy(cm.at[2, rows, :], y.at[2, rows, :], s_h.at[q - 1], r_h.at[0], at(2 * q + d, c))

    def p3_copy(o, q, slot):
        return copy(
            p2sum.at[pl.ds(pl.multiple_of(8 * q, 8), 8), :], p3.at[slot], s_p3.at[o - 1], r_p3.at[slot], at(2 * q + d, c)
        )

    def p4_copy(o, zz, slot):
        rows = pl.ds(pl.multiple_of(32 * c + 8 * slot, 8), 8)
        return copy(pv.at[rows, :], pv.at[rows, :], s_p4.at[o - 1], r_p4.at[slot], at(zz, c))

    def p5_copy(o, cc, slot):
        rows = pl.ds(pl.multiple_of(32 * slot, 32), 32)
        return copy(pv.at[rows, :], pv.at[rows, :], s_p5.at[o - 1], r_p5.at[slot], at(z, cc))

    @pl.when(jnp.logical_not(own))
    def _():
        merge_p().start()
        merge_c().start()

    @pl.when(own)
    def _():
        merge_p().wait_recv()
        pm[...] = pm[...] + pcand[...]
        for o in range(1, 16):
            p2_copy(o, (c + o) % 16, c).start()
        merge_c().wait_recv()
        cm[...] = cm[...] + cand[...]
        for o in range(1, 4):
            rs_copy(o, (z_hi + o) % 4, z_hi).start()

        @pl.when(z_hi == 0)
        def _():
            for q in range(1, 4):
                h_copy(q).start()
            y[2, 0:64, :] = cm[2, 0:64, :]

        total = pm[pl.ds(pl.multiple_of(32 * c, 32), 32), :]
        for o in range(1, 16):
            cc = (c + o) % 16
            p2_copy(o, cc, cc).wait_recv()
            total = total + p2[cc]
        p2sum[...] = total
        for o in range(1, 4):
            p3_copy(o, (z_hi + o) % 4, z_hi).start()
        total = p2sum[pl.ds(pl.multiple_of(8 * z_hi, 8), 8), :]
        for o in range(1, 4):
            q = (z_hi + o) % 4
            p3_copy(o, q, q).wait_recv()
            total = total + p3[q]
        pv[pl.ds(pl.multiple_of(32 * c + 8 * z_hi, 8), 8), :] = total
        for o in range(1, 8):
            p4_copy(o, (z + o) % 8, z_hi).start()
        for o in range(1, 4):
            q = (z_hi + o) % 4
            p4_copy(o, z, q).wait_recv()

    @pl.when(jnp.logical_not(own))
    def _():
        for q in range(4):
            p4_copy(1, z, q).wait_recv()

    for o in range(1, 16):
        p5_copy(o, (c + o) % 16, c).start()

    @pl.when(own)
    def _():
        rows = pl.ds(pl.multiple_of(64 * z_hi, 64), 64)
        total = cm[0:2, rows, :]
        for o in range(1, 4):
            q = (z_hi + o) % 4
            rs_copy(o, q, q).wait_recv()
            total = total + rs[q]
        y[0:2, rows, :] = total

        @pl.when(z_hi != 0)
        def _():
            h_copy(z_hi).wait_recv()

    sign = 1 - 2 * s

    def ag_copy(q, step):
        rows = pl.ds(pl.multiple_of(64 * q, 64), 64)
        send = s_agr if step == 1 else s_agl
        return copy(y.at[:, rows, :], y.at[:, rows, :], send.at[q], r_ag.at[q], at((z + step * sign + 8) % 8, c))

    own_q = z_hi

    def q_at(delta):
        return (((z - sign * delta + 16) % 8 - s) // 2) % 4

    @pl.when(own)
    def _():
        ag_copy(own_q, 1).start()
        ag_copy(own_q, -1).start()
        q2, q6, q4 = q_at(2), q_at(6), q_at(4)
        ag_copy(q2, 1).wait_recv()
        ag_copy(q2, 1).start()
        ag_copy(q6, -1).wait_recv()
        ag_copy(q6, -1).start()
        ag_copy(q4, 1).wait_recv()

    @pl.when(jnp.logical_not(own))
    def _():
        q1, q7, q3, q5 = q_at(1), q_at(7), q_at(3), q_at(5)
        ag_copy(q1, 1).wait_recv()
        ag_copy(q1, 1).start()
        ag_copy(q7, -1).wait_recv()
        ag_copy(q7, -1).start()
        ag_copy(q3, 1).wait_recv()
        ag_copy(q3, 1).start()
        ag_copy(q5, -1).wait_recv()

    def raw_copy(k):
        return copy(
            prior.at[0, pl.ds(pl.multiple_of((1 - d) * 768 + 256 * k, 256), 256), :],
            raw.at[pl.ds(256 * k, 256), :], s_raw.at[k], r_raw.at[k], partner,
        )

    for k in range(3):
        raw_copy(k).start()

    def tree(buf, sends_a, sends_b, recvs, t, p, parts, xs, ys):
        first, count = TREE_ROWS[t]
        count = count // parts
        way = 1 if t % 2 == 0 else -1
        dx = (way * (cx - xs) + 4) % 4
        dy = (way * (cy - ys) + 4) % 4
        depth = dx + dy
        if t < 2:
            to_x = (dy == 0) & (dx < 3)
            to_y = dy < 3
        else:
            to_x = (dy >= 1) & (dx < 3)
            to_y = ((dx == 0) & (dy < 3)) | ((dx >= 1) & (dy == 3))
            depth = depth + jnp.where((dy == 0) & (dx >= 1), 4, 0)
        p = p - depth
        rows = pl.ds(pl.multiple_of(first + (p % parts) * count, 8), count)
        block = buf.at[p // parts, rows, :]
        next_x = at(z, 4 * cy + (cx + way + 4) % 4)
        next_y = at(z, 4 * ((cy + way + 4) % 4) + cx)
        copy_x = copy(block, block, sends_a.at[t, p], recvs.at[t, p], next_x)
        copy_y = copy(block, block, sends_b.at[t, p], recvs.at[t, p], next_y)
        valid = (p >= 0) & (p < buf.shape[0] * parts)
        return valid, depth, to_x, to_y, copy_x, copy_y

    def forward(*args):
        valid, depth, to_x, to_y, copy_x, copy_y = tree(*args)

        @pl.when(valid & (depth > 0))
        def _():
            copy_x.wait_recv()

        @pl.when(valid & to_x)
        def _():
            copy_x.start()

        @pl.when(valid & to_y)
        def _():
            copy_y.start()

    def finish(*args):
        valid, _, to_x, to_y, copy_x, copy_y = tree(*args)

        @pl.when(valid & to_x)
        def _():
            copy_x.wait_send()

        @pl.when(valid & to_y)
        def _():
            copy_y.wait_send()

    k_own = 2 * r + d
    k_sib = 2 * (r + 1 - 2 * s) + d
    xs, ys = k_own % 4, k_own // 4

    def sib_panels(e):
        return copy(y.at[pl.ds(0, 2)], x_out.at[pl.ds(2 * e, 2)], s_sib.at[0], r_sib.at[0], sibling)

    def sib_h():
        return copy(y.at[2], hsib, s_sib.at[1], r_sib.at[1], sibling)

    @pl.when(c == k_sib)
    def _():
        sib_panels(s).start()
        sib_h().start()

    @pl.when(c == 0)
    def _():
        g[...] = y[:, :, 0:TILE]

    g_args = (g, s_ga, s_gb, r_g)

    def g_step(p, carry):
        for t in range(4):
            forward(*g_args, t, p, 1, 0, 0)
        return carry

    lax.fori_loop(0, 3 + 7, g_step, 0)

    @pl.when(c == k_own)
    def _():
        x_out[pl.ds(2 * s, 2)] = y[0:2]
        sib_panels(1 - s).wait_recv()
        sib_h().wait_recv()
        x_out[4] = y[2] + hsib[...]

    x_args = (x_out, s_xa, s_xb, r_x)

    def x_step(p, carry):
        for t in range(4):
            forward(*x_args, t, p, X_PARTS, xs, ys)
        return carry

    lax.fori_loop(0, 5 * X_PARTS + 7, x_step, 0)

    for o in range(1, 16):
        cc = (c + o) % 16
        p5_copy(o, cc, cc).wait_recv()
    for o in range(1, 16):
        p5_copy(o, (c + o) % 16, c).wait_send()

    @pl.when(own)
    def _():
        for o in range(1, 8):
            p4_copy(o, (z + o) % 8, z_hi).wait_send()

    sweep_all(pv)

    gq = g[0:2].reshape(512, TILE)
    us = -dot6(pv[...], gq, ROW_BY_COL)
    u[s] = us
    mparts[s] = g[2] - dot6(gq, us, COL_BY_COL)

    def swap(k, ref, e):
        return copy(ref.at[e], ref.at[e], s_sw.at[k], r_sw.at[k], sibling)

    def swap_r(e):
        return copy(r_out.at[pl.ds(2 * e, 2)], r_out.at[pl.ds(2 * e, 2)], s_sw.at[2], r_sw.at[2], sibling)

    swap(0, u, s).start()
    swap(1, mparts, s).start()

    t0, t1 = piv[s, 0], piv[s, 1]

    def r_step(k, carry):
        cols = pl.ds(pl.multiple_of(k * 256, 256), 256)
        first = c * 768 + k * 256
        ya = modified(y[0, :, cols], t0, t1, first)
        yb = modified(y[1, :, cols], t1, t0, first)
        rk = -dot6(pv[...], jnp.concatenate([ya, yb], axis=0), ROW_BY_COL)
        r_out[2 * s, :, cols] = rk[:TILE]
        r_out[2 * s + 1, :, cols] = rk[TILE:]
        pparts[s, :, cols] = y[2, :, cols] - dot6(gq, rk, COL_BY_COL)
        return carry

    lax.fori_loop(0, 3, r_step, 0)
    swap_r(s).start()
    swap(3, pparts, s).start()

    swap(1, mparts, 1 - s).wait_recv()
    n_out[...] = mparts[0] + mparts[1]
    sweep_all(n_out)

    swap(0, u, 1 - s).wait_recv()

    def p_step(k, carry):
        cols = pl.ds(pl.multiple_of(k * 256, 256), 256)
        first = k_own * 768 + k * 256
        total = x_out[4, :, cols]
        for e in range(2):
            ta, tb = piv[e, 0], piv[e, 1]
            xa = modified(x_out[2 * e, :, cols], ta, tb, first)
            xb = modified(x_out[2 * e + 1, :, cols], tb, ta, first)
            total = total - dot6(u[e], jnp.concatenate([xa, xb], axis=0), COL_BY_COL)
        p0r_out[:, cols] = total
        return carry

    lax.fori_loop(0, 3, p_step, 0)
    swap_r(1 - s).wait_recv()
    swap(3, pparts, 1 - s).wait_recv()
    p0c_out[...] = pparts[0] + pparts[1]

    @pl.when(jnp.logical_not(own))
    def _():
        merge_p().wait_send()
        merge_c().wait_send()
        ag_copy(q_at(1), 1).wait_send()
        ag_copy(q_at(7), -1).wait_send()
        ag_copy(q_at(3), 1).wait_send()

    @pl.when(own)
    def _():
        for o in range(1, 16):
            p2_copy(o, (c + o) % 16, c).wait_send()
        for o in range(1, 4):
            rs_copy(o, (z_hi + o) % 4, z_hi).wait_send()
            p3_copy(o, (z_hi + o) % 4, z_hi).wait_send()

        @pl.when(z_hi == 0)
        def _():
            for q in range(1, 4):
                h_copy(q).wait_send()

        ag_copy(own_q, 1).wait_send()
        ag_copy(own_q, -1).wait_send()
        ag_copy(q_at(2), 1).wait_send()
        ag_copy(q_at(6), -1).wait_send()

    @pl.when(c == k_sib)
    def _():
        sib_panels(s).wait_send()
        sib_h().wait_send()

    def g_end(p, carry):
        for t in range(4):
            finish(*g_args, t, p, 1, 0, 0)
        return carry

    def x_end(p, carry):
        for t in range(4):
            finish(*x_args, t, p, X_PARTS, xs, ys)
        return carry

    lax.fori_loop(0, 3 + 7, g_end, 0)
    lax.fori_loop(0, 5 * X_PARTS + 7, x_end, 0)
    swap(0, u, s).wait_send()
    swap(1, mparts, s).wait_send()
    swap_r(s).wait_send()
    swap(3, pparts, s).wait_send()
    for k in range(3):
        raw_copy(k).wait()


def run_main(cand, pcand, prior, pivots):
    vmem = pl.BlockSpec(memory_space=pltpu.VMEM)
    dma = pltpu.SemaphoreType.DMA
    return pl.pallas_call(
        main_kernel,
        out_shape=(
            jax.ShapeDtypeStruct((768, 768), F32),
            jax.ShapeDtypeStruct((5, 256, 768), F32),
            jax.ShapeDtypeStruct((4, 256, 768), F32),
            jax.ShapeDtypeStruct((256, 768), F32),
            jax.ShapeDtypeStruct((256, 768), F32),
            jax.ShapeDtypeStruct((256, 256), F32),
        ),
        in_specs=[vmem, vmem, pl.BlockSpec(memory_space=pl.ANY), pl.BlockSpec(memory_space=pltpu.SMEM)],
        out_specs=(pl.BlockSpec(memory_space=pl.ANY), vmem, vmem, vmem, vmem, vmem),
        scratch_shapes=[
            pltpu.VMEM((3, 256, 768), F32),
            pltpu.VMEM((512, 512), F32),
            pltpu.VMEM((4, 2, 64, 768), F32),
            pltpu.VMEM((3, 256, 768), F32),
            pltpu.VMEM((256, 768), F32),
            pltpu.VMEM((16, 32, 512), F32),
            pltpu.VMEM((32, 512), F32),
            pltpu.VMEM((4, 8, 512), F32),
            pltpu.VMEM((512, 512), F32),
            pltpu.VMEM((3, 256, 256), F32),
            pltpu.VMEM((2, 512, 256), F32),
            pltpu.VMEM((2, 256, 256), F32),
            pltpu.VMEM((2, 256, 768), F32),
            dma((2,)), dma((2,)),
            dma((15,)), dma((16,)), dma((3,)), dma((4,)), dma((7,)), dma((4,)), dma((15,)), dma((16,)),
            dma((3,)), dma((4,)), dma((3,)), dma((1,)), dma((4,)), dma((4,)), dma((4,)),
            dma((2,)), dma((2,)), dma((4, 3)), dma((4, 3)), dma((4, 3)), dma((4, 5 * X_PARTS)), dma((4, 5 * X_PARTS)), dma((4, 5 * X_PARTS)),
            dma((3,)), dma((3,)), dma((4,)), dma((4,)),
        ],
        compiler_params=pltpu.CompilerParams(
            collective_id=0, has_side_effects=True, vmem_limit_bytes=56 * 1024 * 1024
        ),
    )(cand, pcand, prior, pivots)


def final_kernel(place, piv, own, raw, xt, rr, p0c, p0r, neg, shift, schur, lower):
    step = pl.program_id(0)
    row_first = place[1] * 768 + step * 256
    col_first = place[2] * 768
    rows, cols = row_first + iota((256, 768), 0), col_first + iota((256, 768), 1)
    added = jnp.where(rows == cols, shift[...], 0.0)
    mine = place[0]

    def zeroed(block, e):
        a, b = piv[e, 0], piv[e, 1]
        row_tile, col_tile = rows // TILE, cols // TILE
        hit = (row_tile == a) | (row_tile == b) | (col_tile == a) | (col_tile == b)
        return jnp.where(hit, 0.0, block + added)

    total = zeroed(own[0], mine) + zeroed(raw[...], 1 - mine)
    for e in range(2):
        a, b = piv[e, 0], piv[e, 1]
        xa = modified(xt[2 * e], a, b, row_first)
        xb = modified(xt[2 * e + 1], b, a, row_first)
        x = jnp.concatenate([xa, xb], axis=0)
        y = rr[2 * e : 2 * e + 2].reshape(512, 768)
        total = total - dot3(x, y, COL_BY_COL)
    low = -dot6(p0r[...], neg[...], COL_BY_COL)
    lower[0, 0] = low
    reduced = total - dot3(low, p0c[...], ROW_BY_COL)
    schur[0, 0] = jnp.where((rows < TILE) | (cols < TILE), total, reduced)


def run_final(place, pivots, prior, raw, xt, rr, p0c, p0r, neg, shift):
    whole2 = lambda i, p, v: (0, 0)
    spec = pltpu.PrefetchScalarGridSpec(
        num_scalar_prefetch=2,
        grid=(3,),
        in_specs=[
            pl.BlockSpec((1, 256, 768), lambda i, p, v: (0, 3 * p[0] + i, 0)),
            pl.BlockSpec((256, 768), lambda i, p, v: (i, 0)),
            pl.BlockSpec((5, 256, 256), lambda i, p, v: (0, 0, i)),
            pl.BlockSpec((4, 256, 768), lambda i, p, v: (0, 0, 0)),
            pl.BlockSpec((256, 768), whole2),
            pl.BlockSpec((256, 256), lambda i, p, v: (0, i)),
            pl.BlockSpec((256, 256), whole2),
            pl.BlockSpec((256, 1), lambda i, p, v: (i, 0)),
        ],
        out_specs=(
            pl.BlockSpec((1, 1, 256, 768), lambda i, p, v: (0, 0, i, 0)),
            pl.BlockSpec((1, 1, 256, 256), lambda i, p, v: (0, 0, i, 0)),
        ),
    )
    return pl.pallas_call(
        final_kernel,
        grid_spec=spec,
        out_shape=(
            jax.ShapeDtypeStruct((1, 1, 768, 768), F32),
            jax.ShapeDtypeStruct((1, 1, 768, 256), F32),
        ),
        compiler_params=pltpu.CompilerParams(vmem_limit_bytes=56 * 1024 * 1024),
    )(place, pivots, prior, raw, xt, rr, p0c, p0r, neg, shift)


def shifts(quantum):
    quantum = quantum.astype(F32)
    return (
        0.025 * quantum[:, 0] * (quantum[:, 0] + 1.0)
        + 0.01 * quantum[:, 1] * quantum[:, 1]
        + 0.01 * quantum[:, 2] * (quantum[:, 2] + 1.0)
        + 0.005 * quantum[:, 3] * (quantum[:, 3] + 1.0)
    )


def per_device(prior_y, labels, pivots):
    r, c, d = lax.axis_index("row"), lax.axis_index("col"), lax.axis_index("dir")
    height, width = prior_y.shape[1], prior_y.shape[2]
    row_first, col_first = r * height, c * width
    cols = col_first + jnp.arange(width, dtype=jnp.int32)
    matrix = prior_y[0]

    def tile_rows(tile):
        start = jnp.clip(tile * TILE - row_first, 0, height - TILE)
        block = lax.dynamic_slice_in_dim(matrix, start, TILE, 0)
        shift = shifts(lax.dynamic_slice_in_dim(labels, tile * TILE, TILE, 0))
        ids = tile * TILE + jnp.arange(TILE, dtype=jnp.int32)
        block = block + jnp.where(ids[:, None] == cols[None, :], shift[:, None], 0.0)
        return jnp.where(tile * TILE // height == r, block, 0.0)

    ta, tb = pivots[d, 0], pivots[d, 1]
    first, second, lead = tile_rows(ta), tile_rows(tb), tile_rows(jnp.int32(0))
    gone = (cols // TILE == ta) | (cols // TILE == tb)
    lead = jnp.where(gone[None, :], 0.0, lead)
    cand = jnp.stack([first, second, lead])

    def tile_cols(tile):
        start = jnp.clip(tile * TILE - col_first, 0, width - TILE)
        block = lax.dynamic_slice_in_dim(cand[:2], start, TILE, 2).reshape(2 * TILE, TILE)
        return jnp.where(tile * TILE // width == c, block, 0.0)

    pcand = jnp.concatenate([tile_cols(ta), tile_cols(tb)], axis=1)
    raw, xt, rr, p0c, p0r, neg = run_main(cand, pcand, prior_y, pivots)
    shift = shifts(lax.dynamic_slice_in_dim(labels, row_first + d * 768, 768, 0))[:, None]
    place = jnp.stack([d, 2 * r + d, c]).astype(jnp.int32)
    return run_final(place, pivots, prior_y, raw, xt, rr, p0c, p0r, neg, shift)


def solution(mesh):
    placed = (P("dir", "row", "col"), P(), P())
    return jax.shard_map(
        per_device,
        mesh=mesh,
        in_specs=placed,
        out_specs=(P("row", "dir", None, "col"), P("row", "dir", None, None)),
        check_vma=False,
    )
```

time: 962 us -> 262 us (0.27)
  the two profiles are of different devices: /device:TPU:74 before, /device:TPU:32 now
where the time goes in v1:
time: 262 us; the launch traced here: 261 us
  Pallas kernels  248 us (95%)
  other arithmetic  9.15 us (3%)
    pallas_call x1, Pallas kernels, run_main(): pl.pallas_call(main_kernel, out_shape=(jax.ShapeDtypeStruct((768, 768), F...  235 us
    pallas_call x1, Pallas kernels, run_final(): pl.pallas_call(final_kernel, grid_spec=spec, out_shape=(jax.ShapeDtypeStr...  12.5 us

profile of v1, /device:TPU:32, one launch (start us, length us, event | category | flops | bytes accessed | tf_op | source)
XLA Modules:
  0.0 261.4 jit_solution(5611618153173924050)
XLA Ops:
  0.6 1.4 constant_dynamic-slice_fusion.1
  3.4 0.7 dynamic-slice_convert_fusion.1
  4.3 1.3 compare_or_fusion
  5.6 2.2 add_select_fusion.1
  8.0 0.3 fusion.3
  8.3 1.1 pad_maximum_fusion.1.pcand
  9.4 1.6 pad_maximum_fusion.cand
  11.0 235.2 %shard_map.50 = (f32[768,768]{1,0:T(8,128)}, f32[5,256,768]{2,1,0:T(8,128)}, f32[4,256,768]{2,1,0:T(8,128)}, f32[256,768]{1,0:T(8,128)}, f32[256,768]{1,0:T(8,128)}, /*index=5*/f32[256,256]{1,0:T(8,128)}) custom-call(f32[3,256,768]{2,1,0:T(8,128)} %pad_maximum_fusion.cand, f32[512,512]{1,0:T(8,128)} %pad_maximum_fusion.1.pcand, f32[1,1536,768]{2,1,0:T(8,128)} %own.1, ...), custom_call_target="tpu_custom_call" | custom-call | tf_op jit(solution)/shard_map/pallas_call | solution.py:504
  246.2 0.7 constant_dynamic-slice_fusion
  246.9 0.2 copy.8
  247.2 1.1 fusion.6.shift
  248.3 0.6 pad_add_fusion.place
  248.9 12.5 %shard_map.51 = (f32[1,1,768,768]{3,2,1,0:T(8,128)}, f32[1,1,768,256]{3,2,1,0:T(8,128)}) custom-call(s32[3]{0:T(128)} %pad_add_fusion.place, s32[2,2]{1,0:T(2,128)} %piv.3, f32[1,1536,768]{2,1,0:T(8,128)} %own.1, f32[768,768]{1,0:T(8,128)} %get-tuple-element.8.raw, f32[5,256,768]{2,1,0:T(8,128)} %get-tuple-element.9.xt, ...), custom_call_target="tpu_custom_call" | custom-call | tf_op jit(solution)/shard_map/pallas_call | solution.py:590
  (5 shorter events, 0.1 us)

commit v2 on v1

v2 whole, which is shorter than its diff:
```python
import functools

import jax
import jax.numpy as jnp
from jax import lax
from jax.experimental import pallas as pl
from jax.experimental.pallas import tpu as pltpu
from jax.sharding import PartitionSpec as P

TILE = 256
F32 = jnp.float32
BF16 = jnp.bfloat16
MESH = pl.DeviceIdType.MESH
ROW_BY_COL = ((1,), (0,))
COL_BY_COL = ((0,), (0,))


def dot6(a, b, dims):
    return lax.dot_general(
        a, b, (dims, ((), ())), precision=lax.Precision.HIGHEST, preferred_element_type=F32
    )


def split(x):
    high = x.astype(BF16)
    return high, (x - high.astype(F32)).astype(BF16)


def dot3(a, b, dims):
    ah, al = split(a)
    bh, bl = split(b)

    def one(p, q):
        return lax.dot_general(p, q, (dims, ((), ())), preferred_element_type=F32)

    return one(ah, bh) + (one(ah, bl) + one(al, bh))


def iota(shape, dim):
    return lax.broadcasted_iota(jnp.int32, shape, dim)


def sweep128(block, service, group=4):
    lanes, subs = iota((8, 128), 1), iota((8, 128), 0)
    width = 8 * group
    hits = [subs == k for k in range(8)]

    def body(step, b):
        service(step)
        s = [b[8 * j : 8 * j + 8, :] for j in range(group)]
        for i in range(group):
            v = [jnp.broadcast_to(s[i][:, 8 * i + m : 8 * i + m + 1], (8, 128)) for m in range(8)]
            for k in range(8):
                vk = v[k]
                inv = 1.0 / vk[k : k + 1, :]
                for j in range(8):
                    if j != k:
                        rj = v[j][k : k + 1, :] * inv
                        v[j] = jnp.where(hits[k], rj, v[j] - vk * rj)
                v[k] = jnp.where(hits[k], -inv, vk * inv)
            inside = (lanes >= 8 * i) & (lanes < 8 * i + 8)
            x = jnp.where(inside, jnp.where(lanes - 8 * i == subs, -1.0, 0.0), s[i])
            r = -v[0] * x[0:1, :]
            for m in range(1, 8):
                r = r - v[m] * x[m : m + 1, :]
            for q in range(1, group):
                j = (i + q) % group
                acc = jnp.where(inside, 0.0, s[j])
                for m in range(8):
                    col = jnp.broadcast_to(s[j][:, 8 * i + m : 8 * i + m + 1], (8, 128))
                    acc = acc - col * r[m : m + 1, :]
                s[j] = acc
            s[i] = r
        r = jnp.concatenate(s, axis=0)
        rest = b[width:, :]
        lane = iota(rest.shape, 1)
        rest = jnp.where(lane < width, 0.0, rest) - dot6(rest[:, :width], r, ROW_BY_COL)
        return pltpu.roll(jnp.concatenate([rest, r], axis=0), 128 - width, 1)

    return lax.fori_loop(0, 128 // width, body, block)


def sweep_step(a_ref, p, service):
    n = a_ref.shape[0]
    at = pl.multiple_of(p * 128, 128)
    neg = sweep128(a_ref[pl.ds(at, 128), pl.ds(at, 128)], service)
    x = a_ref[pl.ds(at, 128), :]
    col, row = iota((128, n), 1), iota((128, n), 0)
    x = jnp.where(col // 128 == p, jnp.where(col - at == row, -1.0, 0.0), x)
    r = -dot6(neg, x, ROW_BY_COL)
    a_ref[pl.ds(at, 128), :] = jnp.zeros((128, n), F32)
    a_ref[:, pl.ds(at, 128)] = jnp.zeros((n, 128), F32)
    a_ref[...] = a_ref[...] - dot6(x, r, COL_BY_COL)


def modified(panel, tile, other, col_first):
    ids = col_first + iota(panel.shape, 1)
    local = ids - tile * TILE
    own = (local >= 0) & (local < TILE)
    beside = ids - other * TILE
    gone = (beside >= 0) & (beside < TILE)
    panel = jnp.where(own, jnp.where(local == iota(panel.shape, 0), -1.0, 0.0), panel)
    return jnp.where(gone, 0.0, panel)


def main_kernel(
    a_ref, shift, prior, piv,
    raw, corr, low_out,
    x_buf, r_buf, p0c_buf, n_buf, cand, pcand, cm, pm, rs, y, hpre, p2, p2sum, p3, pv, gr, gsum, gp, g, u, mparts, pparts,
    sem_p1, sem_c1, sem_h1, s_p2, r_p2, s_p3, r_p3, s_p4, r_p4, s_p5, r_p5,
    s_g1, r_g1, s_g2, r_g2, s_g3, r_g3, s_g4, r_g4,
    s_rs, r_rs, s_h, r_h, s_agr, s_agl, r_ag, s_ahr, s_ahl, r_ah,
    s_sib, r_sib, s_sibh, r_sibh, s_xa, s_xb, r_x, s_raw, r_raw, s_sw, r_sw,
):
    d, r, c = lax.axis_index("dir"), lax.axis_index("row"), lax.axis_index("col")
    s, z_hi = r % 2, r // 2
    z = 2 * z_hi + d
    cx, cy = c % 4, c // 4
    own = s == d
    other = s != d

    def at(zz, cc):
        return (zz % 2, 2 * (zz // 2) + s, cc)

    sibling = (d, r + 1 - 2 * s, c)
    partner = (1 - d, r, c)

    def copy(src, dst, send, recv, device):
        return pltpu.make_async_remote_copy(
            src_ref=src, dst_ref=dst, send_sem=send, recv_sem=recv, device_id=device, device_id_type=MESH
        )

    def span(first, count):
        return pl.ds(pl.multiple_of(first, 8), count)

    barrier = pltpu.get_barrier_semaphore()
    pl.semaphore_signal(barrier, inc=1, device_id=sibling, device_id_type=MESH)
    for o in range(1, 8):
        pl.semaphore_signal(barrier, inc=1, device_id=at((z + o) % 8, c), device_id_type=MESH)
    for o in range(1, 16):
        pl.semaphore_signal(barrier, inc=1, device_id=at(z, (c + o) % 16), device_id_type=MESH)

    tiles = (piv[d, 0], piv[d, 1])
    col_ids = c * 768 + iota((TILE, 768), 1)
    for k in range(2):
        named = jnp.full((TILE, 768), tiles[k], jnp.int32)
        block = jnp.zeros((TILE, 768), F32)
        for j in range(6):
            block = jnp.where(named == 6 * r + j, a_ref[0, TILE * j : TILE * j + TILE, :], block)
        ids = tiles[k] * TILE + iota((TILE, 768), 0)
        here = (ids == col_ids) & (ids >= r * 1536) & (ids < r * 1536 + 1536)
        cand[k] = block + jnp.where(here, shift[...], 0.0)
    lead = a_ref[0, 0:TILE, :] + jnp.where(iota((TILE, 768), 0) == col_ids, shift[...], 0.0)
    gone = (col_ids // TILE == tiles[0]) | (col_ids // TILE == tiles[1]) | (iota((TILE, 768), 0) + r * 1536 >= 1536)
    cand[2] = jnp.where(gone, 0.0, lead)
    for k in range(2):
        named = jnp.full((2 * TILE, TILE), tiles[k], jnp.int32)
        block = jnp.zeros((2 * TILE, TILE), F32)
        for j in range(3):
            part = cand[0:2, :, TILE * j : TILE * j + TILE].reshape(2 * TILE, TILE)
            block = jnp.where(named == 3 * c + j, part, block)
        pcand[:, TILE * k : TILE * k + TILE] = block
    pl.semaphore_wait(barrier, 23)

    def merge_p():
        return copy(pcand, pm, sem_p1.at[0], sem_p1.at[1], sibling)

    def merge_c():
        return copy(cand.at[pl.ds(0, 2)], cm.at[pl.ds(0, 2)], sem_c1.at[0], sem_c1.at[1], sibling)

    def h_first():
        return copy(cand.at[2], hpre, sem_h1.at[0], sem_h1.at[1], partner)

    def p2_copy(o, cc, slot):
        return copy(pm.at[span(32 * cc, 32), :], p2.at[slot], s_p2.at[o - 1], r_p2.at[slot], at(z, cc))

    def rs_copy(o, q, slot):
        return copy(
            cm.at[pl.ds(0, 2), span(64 * q, 64), :], rs.at[slot], s_rs.at[o - 1], r_rs.at[slot], at(2 * q + d, c)
        )

    def h_copy(q):
        rows = span(64 * q, 64)
        return copy(cm.at[2, rows, :], y.at[2, rows, :], s_h.at[q - 1], r_h.at[0], at(2 * q + d, c))

    def p3_copy(o, q, slot):
        return copy(p2sum.at[span(8 * q, 8), :], p3.at[slot], s_p3.at[o - 1], r_p3.at[slot], at(2 * q + d, c))

    def p4_copy(o, zz, slot):
        rows = span(32 * c + 8 * slot, 8)
        return copy(pv.at[rows, :], pv.at[rows, :], s_p4.at[o - 1], r_p4.at[slot], at(zz, c))

    def p5_copy(o, cc, slot):
        rows = span(32 * slot, 32)
        return copy(pv.at[rows, :], pv.at[rows, :], s_p5.at[o - 1], r_p5.at[slot], at(z, cc))

    def g1_copy(o, q, slot):
        return copy(
            cm.at[:, span(64 * q, 64), pl.ds(0, TILE)], gr.at[slot], s_g1.at[o - 1], r_g1.at[slot], at(2 * q + d, c)
        )

    def g2_copy(cc):
        return copy(
            gsum.at[:, span(8 * cc, 8), :], gp.at[cc, :, span(8 * z_hi, 8), :], s_g2.at[cc - 1], r_g2.at[0], at(z, cc)
        )

    def g3_copy(o, zz, slot):
        block = gp.at[c, :, span(8 * slot, 8), :]
        return copy(block, block, s_g3.at[o - 1], r_g3.at[slot], at(zz, c))

    def g4_copy(o, cc, slot):
        return copy(gp.at[slot], gp.at[slot], s_g4.at[o - 1], r_g4.at[slot], at(z, cc))

    def raw_copy(k):
        return copy(
            prior.at[0, span((1 - d) * 768 + 256 * k, 256), :],
            raw.at[pl.ds(256 * k, 256), :], s_raw.at[k], r_raw.at[k], partner,
        )

    sends_h = (d == 1) & (r == 0)
    leads_h = (d == 0) & (r == 0)

    @pl.when(other)
    def _():
        merge_p().start()
        merge_c().start()

    @pl.when(sends_h)
    def _():
        h_first().start()

    @pl.when(s == 1)
    def _():
        y[2] = jnp.zeros((TILE, 768), F32)

    def push_g4():
        @pl.when(c < 8)
        def _():
            for o in range(1, 16):
                g4_copy(o, (c + o) % 16, c).start()

    @pl.when(own)
    def _():
        merge_p().wait_recv()
        pm[...] = pm[...] + pcand[...]
        for o in range(1, 16):
            p2_copy(o, (c + o) % 16, c).start()
        merge_c().wait_recv()
        cm[0:2] = cm[0:2] + cand[0:2]

        @pl.when(leads_h)
        def _():
            h_first().wait_recv()
            cm[2] = cand[2] + hpre[...]

        @pl.when(r != d)
        def _():
            cm[2] = jnp.zeros((TILE, 768), F32)

        @pl.when((r == d) & (d == 1))
        def _():
            cm[2] = jnp.zeros((TILE, 768), F32)

        @pl.when(c == 0)
        def _():
            for o in range(1, 4):
                g1_copy(o, (z_hi + o) % 4, z_hi).start()

        for o in range(1, 4):
            rs_copy(o, (z_hi + o) % 4, z_hi).start()

        @pl.when(leads_h)
        def _():
            for q in range(1, 4):
                h_copy(q).start()
            y[2, 0:64, :] = cm[2, 0:64, :]

        total = pm[span(32 * c, 32), :]
        for o in range(1, 16):
            cc = (c + o) % 16
            p2_copy(o, cc, cc).wait_recv()
            total = total + p2[cc]
        p2sum[...] = total
        for o in range(1, 4):
            p3_copy(o, (z_hi + o) % 4, z_hi).start()

        @pl.when(c == 0)
        def _():
            total = cm[:, span(64 * z_hi, 64), 0:TILE]
            for o in range(1, 4):
                q = (z_hi + o) % 4
                g1_copy(o, q, q).wait_recv()
                total = total + gr[q]
            gsum[...] = total
            for cc in range(1, 8):
                g2_copy(cc).start()
            gp[0, :, span(8 * z_hi, 8), :] = total[:, 0:8]

        total = p2sum[span(8 * z_hi, 8), :]
        for o in range(1, 4):
            q = (z_hi + o) % 4
            p3_copy(o, q, q).wait_recv()
            total = total + p3[q]
        pv[span(32 * c + 8 * z_hi, 8), :] = total
        for o in range(1, 8):
            p4_copy(o, (z + o) % 8, z_hi).start()

        @pl.when((c > 0) & (c < 8))
        def _():
            g2_copy(c).wait_recv()

        @pl.when(c < 8)
        def _():
            for o in range(1, 8):
                g3_copy(o, (z + o) % 8, z_hi).start()

        for o in range(1, 4):
            q = (z_hi + o) % 4
            p4_copy(o, z, q).wait_recv()

    @pl.when(other)
    def _():
        for q in range(4):
            p4_copy(1, z, q).wait_recv()

    for o in range(1, 16):
        p5_copy(o, (c + o) % 16, c).start()

    def order(e, k):
        delta = jnp.where(
            e == d,
            jnp.where(k == 0, 0, jnp.where(k == 1, 2, jnp.where(k == 2, 6, 4))),
            jnp.where(k == 0, 1, jnp.where(k == 1, 7, jnp.where(k == 2, 3, 5))),
        )
        return (((z - (1 - 2 * e) * delta + 16) % 8 - e + 8) // 2) % 4

    class Ring:
        def __init__(self, k, step):
            q = order(s, k)
            rows = span(64 * q, 64)
            right = step == 1
            to = at((z + step * (1 - 2 * s) + 8) % 8, c)
            block = y.at[pl.ds(0, 2), rows, :]
            self.main = copy(block, block, (s_agr if right else s_agl).at[q], r_ag.at[q], to)
            block = y.at[2, rows, :]
            self.lead = copy(block, block, (s_ahr if right else s_ahl).at[q], r_ah.at[q], to)

        def both(self, name):
            getattr(self.main, name)()

            @pl.when(s == 0)
            def _():
                getattr(self.lead, name)()

    def arrive(k):
        Ring(k, 1).both("wait_recv")

    def stage(k):
        if k == 0 or k == 2:
            @pl.when(other)
            def _():
                arrive(k)
                Ring(k, 1).both("start")
                arrive(k + 1)
                if k == 0:
                    Ring(k + 1, -1).both("start")
        elif k == 1:
            @pl.when(own)
            def _():
                arrive(1)
                Ring(1, 1).both("start")
                arrive(2)
                Ring(2, -1).both("start")
        else:
            @pl.when(own)
            def _():
                arrive(3)

    @pl.when(own)
    def _():
        rows = span(64 * z_hi, 64)
        total = cm[0:2, rows, :]
        for o in range(1, 4):
            q = (z_hi + o) % 4
            rs_copy(o, q, q).wait_recv()
            total = total + rs[q]
        y[0:2, rows, :] = total

        @pl.when((d == 0) & (r != 0))
        def _():
            h_copy(z_hi).wait_recv()

        Ring(0, 1).both("start")
        Ring(0, -1).both("start")

    k_own = 2 * r + d
    k_sib = 2 * (r + 1 - 2 * s) + d
    xs, ys = k_own % 4, k_own // 4

    def sib_panels(e, k):
        rows = span(64 * order(e, k), 64)
        return copy(
            y.at[pl.ds(0, 2), rows, :], x_buf.at[pl.ds(2 * e, 2), rows, :], s_sib.at[k], r_sib.at[k], sibling
        )

    def sib_h(k):
        rows = span(64 * order(0, k), 64)
        return copy(y.at[2, rows, :], x_buf.at[4, rows, :], s_sibh.at[k], r_sibh.at[k], sibling)

    def to_root(k):
        @pl.when(c == k_sib)
        def _():
            sib_panels(s, k).start()

            @pl.when(s == 0)
            def _():
                sib_h(k).start()

        @pl.when(c == k_own)
        def _():
            rows = span(64 * order(s, k), 64)
            x_buf[pl.ds(2 * s, 2), rows, :] = y[0:2, rows, :]

            @pl.when(s == 0)
            def _():
                x_buf[4, rows, :] = y[2, rows, :]

            sib_panels(1 - s, k).wait_recv()

            @pl.when(s == 1)
            def _():
                sib_h(k).wait_recv()

    def tree(t, slot):
        way = 1 if t % 2 == 0 else -1
        dx = (way * (cx - xs) + 4) % 4
        dy = (way * (cy - ys) + 4) % 4
        depth = dx + dy
        if t < 2:
            to_x = (dy == 0) & (dx < 3)
            to_y = dy < 3
        else:
            to_x = (dy >= 1) & (dx < 3)
            to_y = ((dx == 0) & (dy < 3)) | ((dx >= 1) & (dy == 3))
            depth = depth + jnp.where((dy == 0) & (dx >= 1), 4, 0)
        p = slot - 2 * depth
        valid = (p >= 0) & (p < 20)
        p = jnp.where(valid, p, 0)
        tile = p % 5
        rows = span(64 * order(jnp.where(tile == 4, 0, tile // 2), p // 5) + 16 * t, 16)
        block = x_buf.at[tile, rows, :]
        next_x = at(z, 4 * cy + (cx + way + 4) % 4)
        next_y = at(z, 4 * ((cy + way + 4) % 4) + cx)
        copy_x = copy(block, block, s_xa.at[t, p], r_x.at[t, p], next_x)
        copy_y = copy(block, block, s_xb.at[t, p], r_x.at[t, p], next_y)
        return valid, depth, to_x, to_y, copy_x, copy_y

    def x_slot(slot):
        for t in range(4):
            valid, depth, to_x, to_y, copy_x, copy_y = tree(t, slot)

            @pl.when(valid & (depth > 0))
            def _():
                copy_x.wait_recv()

            @pl.when(valid & to_x)
            def _():
                copy_x.start()

            @pl.when(valid & to_y)
            def _():
                copy_y.start()

    def x_end(slot):
        for t in range(4):
            valid, _, to_x, to_y, copy_x, copy_y = tree(t, slot)

            @pl.when(valid & to_x)
            def _():
                copy_x.wait_send()

            @pl.when(valid & to_y)
            def _():
                copy_y.wait_send()

    for o in range(1, 16):
        cc = (c + o) % 16
        p5_copy(o, cc, cc).wait_recv()
    for o in range(1, 16):
        p5_copy(o, (c + o) % 16, c).wait_send()

    @pl.when(own & (c < 8))
    def _():
        for o in range(1, 4):
            q = (z_hi + o) % 4
            g3_copy(o, z, q).wait_recv()

    @pl.when(other & (c < 8))
    def _():
        for q in range(4):
            g3_copy(1, z, q).wait_recv()

    push_g4()

    @pl.when(own)
    def _():
        for o in range(1, 8):
            p4_copy(o, (z + o) % 8, z_hi).wait_send()

    def outer(p, carry):
        sweep_step(pv, p, lambda i: x_slot(5 * (p - 1) + i))
        x_slot(5 * (p - 1) + 4)
        for k in range(4):
            @pl.when(p == k)
            def _():
                stage(k)
        to_root(p)

        @pl.when(p == 2)
        def _():
            raw_copy(0).start()

        return carry

    lax.fori_loop(0, 4, outer, 0)
    raw_copy(1).start()
    raw_copy(2).start()

    for o in range(1, 16):
        cc = (c + o) % 16

        @pl.when(cc < 8)
        def _():
            g4_copy(o, cc, jnp.where(cc < 8, cc, 0)).wait_recv()

    for k in range(3):
        for q in range(4):
            for cc in range(8):
                g[k, 64 * q + 8 * cc : 64 * q + 8 * cc + 8, :] = gp[cc, k, 8 * q : 8 * q + 8, :]

    x_slot(15)
    gq = g[0:2].reshape(512, TILE)
    us = -dot6(pv[...], gq, ROW_BY_COL)
    u[s] = us
    mparts[s] = g[2] - dot6(gq, us, COL_BY_COL)

    def swap(k, ref, e):
        return copy(ref.at[e], ref.at[e], s_sw.at[k], r_sw.at[k], sibling)

    def swap_r(e):
        return copy(r_buf.at[pl.ds(2 * e, 2)], r_buf.at[pl.ds(2 * e, 2)], s_sw.at[2], r_sw.at[2], sibling)

    swap(1, mparts, s).start()
    swap(0, u, s).start()
    x_slot(16)

    t0, t1 = piv[s, 0], piv[s, 1]

    def r_step(k, carry):
        cols = pl.ds(pl.multiple_of(k * 256, 256), 256)
        first = c * 768 + k * 256
        ya = modified(y[0, :, cols], t0, t1, first)
        yb = modified(y[1, :, cols], t1, t0, first)
        rk = -dot6(pv[...], jnp.concatenate([ya, yb], axis=0), ROW_BY_COL)
        r_buf[2 * s, :, cols] = rk[:TILE]
        r_buf[2 * s + 1, :, cols] = rk[TILE:]
        pparts[s, :, cols] = y[2, :, cols] - dot6(g[0:2].reshape(512, TILE), rk, COL_BY_COL)
        x_slot(17 + k)
        return carry

    lax.fori_loop(0, 3, r_step, 0)
    swap_r(s).start()
    swap(3, pparts, s).start()

    swap(1, mparts, 1 - s).wait_recv()
    n_buf[...] = mparts[0] + mparts[1]

    def outer_lead(p, carry):
        def two_slots(i):
            k = 4 * p + i
            first, last = (7 * k) // 4, (7 * (k + 1)) // 4
            x_slot(20 + first)
            x_slot(jnp.where(last - first == 2, 21 + first, -1))

        sweep_step(n_buf, p, two_slots)
        return carry

    lax.fori_loop(0, 2, outer_lead, 0)
    swap(0, u, 1 - s).wait_recv()

    swap_r(1 - s).wait_recv()
    swap(3, pparts, 1 - s).wait_recv()
    p0c_buf[...] = pparts[0] + pparts[1]

    def last_step(k, carry):
        cols = pl.ds(pl.multiple_of(k * 256, 256), 256)
        rows = span(k * 256, 256)
        first = k_own * 768 + k * 256
        lead = x_buf[4, :, cols]
        total = jnp.zeros((TILE, 768), F32)
        for e in range(2):
            ta, tb = piv[e, 0], piv[e, 1]
            xa = modified(x_buf[2 * e, :, cols], ta, tb, first)
            xb = modified(x_buf[2 * e + 1, :, cols], tb, ta, first)
            x = jnp.concatenate([xa, xb], axis=0)
            lead = lead - dot6(u[e], x, COL_BY_COL)
            total = total - dot3(x, r_buf[2 * e : 2 * e + 2].reshape(512, 768), COL_BY_COL)
        low = -dot6(lead, n_buf[...], COL_BY_COL)
        low_out[rows, :] = low
        keep = (first + iota((TILE, 768), 0) < TILE) | (col_ids < TILE)
        corr[rows, :] = total - jnp.where(keep, 0.0, dot3(low, p0c_buf[...], ROW_BY_COL))
        return carry

    lax.fori_loop(0, 3, last_step, 0)

    @pl.when(other)
    def _():
        merge_p().wait_send()
        merge_c().wait_send()
        Ring(0, 1).both("wait_send")
        Ring(1, -1).both("wait_send")
        Ring(2, 1).both("wait_send")

    @pl.when(sends_h)
    def _():
        h_first().wait_send()

    @pl.when(own)
    def _():
        for o in range(1, 16):
            p2_copy(o, (c + o) % 16, c).wait_send()
        for o in range(1, 4):
            rs_copy(o, (z_hi + o) % 4, z_hi).wait_send()
            p3_copy(o, (z_hi + o) % 4, z_hi).wait_send()

        @pl.when(leads_h)
        def _():
            for q in range(1, 4):
                h_copy(q).wait_send()

        @pl.when(c == 0)
        def _():
            for o in range(1, 4):
                g1_copy(o, (z_hi + o) % 4, z_hi).wait_send()
            for cc in range(1, 8):
                g2_copy(cc).wait_send()

        @pl.when(c < 8)
        def _():
            for o in range(1, 8):
                g3_copy(o, (z + o) % 8, z_hi).wait_send()

        Ring(0, 1).both("wait_send")
        Ring(0, -1).both("wait_send")
        Ring(1, 1).both("wait_send")
        Ring(2, -1).both("wait_send")

    @pl.when(c < 8)
    def _():
        for o in range(1, 16):
            g4_copy(o, (c + o) % 16, c).wait_send()

    @pl.when(c == k_sib)
    def _():
        for k in range(4):
            sib_panels(s, k).wait_send()

            @pl.when(s == 0)
            def _():
                sib_h(k).wait_send()

    def x_last(slot, carry):
        x_end(slot)
        return carry

    lax.fori_loop(0, 34, x_last, 0)
    swap(0, u, s).wait_send()
    swap(1, mparts, s).wait_send()
    swap_r(s).wait_send()
    swap(3, pparts, s).wait_send()
    for k in range(3):
        raw_copy(k).wait()


def run_main(prior, shift, pivots):
    vmem = pl.BlockSpec(memory_space=pltpu.VMEM)
    dma = pltpu.SemaphoreType.DMA
    return pl.pallas_call(
        main_kernel,
        out_shape=(
            jax.ShapeDtypeStruct((768, 768), F32),
            jax.ShapeDtypeStruct((768, 768), F32),
            jax.ShapeDtypeStruct((768, 256), F32),
        ),
        in_specs=[vmem, vmem, pl.BlockSpec(memory_space=pl.ANY), pl.BlockSpec(memory_space=pltpu.SMEM)],
        out_specs=(pl.BlockSpec(memory_space=pl.ANY), vmem, vmem),
        scratch_shapes=[
            pltpu.VMEM((5, 256, 768), F32),
            pltpu.VMEM((4, 256, 768), F32),
            pltpu.VMEM((256, 768), F32),
            pltpu.VMEM((256, 256), F32),
            pltpu.VMEM((3, 256, 768), F32),
            pltpu.VMEM((512, 512), F32),
            pltpu.VMEM((3, 256, 768), F32),
            pltpu.VMEM((512, 512), F32),
            pltpu.VMEM((4, 2, 64, 768), F32),
            pltpu.VMEM((3, 256, 768), F32),
            pltpu.VMEM((256, 768), F32),
            pltpu.VMEM((16, 32, 512), F32),
            pltpu.VMEM((32, 512), F32),
            pltpu.VMEM((4, 8, 512), F32),
            pltpu.VMEM((512, 512), F32),
            pltpu.VMEM((4, 3, 64, 256), F32),
            pltpu.VMEM((3, 64, 256), F32),
            pltpu.VMEM((8, 3, 32, 256), F32),
            pltpu.VMEM((3, 256, 256), F32),
            pltpu.VMEM((2, 512, 256), F32),
            pltpu.VMEM((2, 256, 256), F32),
            pltpu.VMEM((2, 256, 768), F32),
            dma((2,)), dma((2,)), dma((2,)),
            dma((15,)), dma((16,)), dma((3,)), dma((4,)), dma((7,)), dma((4,)), dma((15,)), dma((16,)),
            dma((3,)), dma((4,)), dma((7,)), dma((1,)), dma((7,)), dma((4,)), dma((15,)), dma((8,)),
            dma((3,)), dma((4,)), dma((3,)), dma((1,)),
            dma((4,)), dma((4,)), dma((4,)), dma((4,)), dma((4,)), dma((4,)),
            dma((4,)), dma((4,)), dma((4,)), dma((4,)),
            dma((4, 20)), dma((4, 20)), dma((4, 20)),
            dma((3,)), dma((3,)), dma((4,)), dma((4,)),
        ],
        compiler_params=pltpu.CompilerParams(
            collective_id=0, has_side_effects=True, vmem_limit_bytes=56 * 1024 * 1024
        ),
    )(prior, shift, prior, pivots)


def final_kernel(place, piv, own, raw, corr, low, shift, schur, lower):
    step = pl.program_id(0)
    rows = place[1] * 768 + step * 256 + iota((256, 768), 0)
    cols = place[2] * 768 + iota((256, 768), 1)
    added = jnp.where(rows == cols, shift[...], 0.0)
    row_tile, col_tile = rows // TILE, cols // TILE

    def zeroed(block, e):
        a, b = piv[e, 0], piv[e, 1]
        hit = (row_tile == a) | (row_tile == b) | (col_tile == a) | (col_tile == b)
        return jnp.where(hit, 0.0, block + added)

    schur[0, 0] = zeroed(own[0], place[0]) + zeroed(raw[...], 1 - place[0]) + corr[...]
    lower[0, 0] = low[...]


def run_final(place, pivots, prior, raw, corr, low, shift):
    spec = pltpu.PrefetchScalarGridSpec(
        num_scalar_prefetch=2,
        grid=(3,),
        in_specs=[
            pl.BlockSpec((1, 256, 768), lambda i, p, v: (0, 3 * p[0] + i, 0)),
            pl.BlockSpec((256, 768), lambda i, p, v: (i, 0)),
            pl.BlockSpec((256, 768), lambda i, p, v: (i, 0)),
            pl.BlockSpec((256, 256), lambda i, p, v: (i, 0)),
            pl.BlockSpec((1, 768), lambda i, p, v: (0, 0)),
        ],
        out_specs=(
            pl.BlockSpec((1, 1, 256, 768), lambda i, p, v: (0, 0, i, 0)),
            pl.BlockSpec((1, 1, 256, 256), lambda i, p, v: (0, 0, i, 0)),
        ),
    )
    return pl.pallas_call(
        final_kernel,
        grid_spec=spec,
        out_shape=(
            jax.ShapeDtypeStruct((1, 1, 768, 768), F32),
            jax.ShapeDtypeStruct((1, 1, 768, 256), F32),
        ),
        compiler_params=pltpu.CompilerParams(vmem_limit_bytes=56 * 1024 * 1024),
    )(place, pivots, prior, raw, corr, low, shift)


def shifts(quantum):
    quantum = quantum.astype(F32)
    return (
        0.025 * quantum[:, 0] * (quantum[:, 0] + 1.0)
        + 0.01 * quantum[:, 1] * quantum[:, 1]
        + 0.01 * quantum[:, 2] * (quantum[:, 2] + 1.0)
        + 0.005 * quantum[:, 3] * (quantum[:, 3] + 1.0)
    )


def per_device(prior_y, labels, pivots):
    r, c, d = lax.axis_index("row"), lax.axis_index("col"), lax.axis_index("dir")
    shift = shifts(lax.dynamic_slice_in_dim(labels, c * 768, 768, 0))[None, :]
    raw, corr, low = run_main(prior_y, shift, pivots)
    place = jnp.stack([d, 2 * r + d, c]).astype(jnp.int32)
    return run_final(place, pivots, prior_y, raw, corr, low, shift)


def solution(mesh):
    placed = (P("dir", "row", "col"), P(), P())
    return jax.shard_map(
        per_device,
        mesh=mesh,
        in_specs=placed,
        out_specs=(P("row", "dir", None, "col"), P("row", "dir", None, None)),
        check_vma=False,
    )
```

time: 262 us -> 185 us (0.71)
  the two profiles are of different devices: /device:TPU:32 before, /device:TPU:74 now
where the time goes in v2:
time: 185 us; the launch traced here: 182 us
  Pallas kernels  179 us (97%)
  other arithmetic  1.91 us (1%)
    pallas_call x1, Pallas kernels, run_main(): pl.pallas_call(main_kernel, out_shape=(jax.ShapeDtypeStruct((768, 768), F...  172 us
    pallas_call x1, Pallas kernels, run_final(): pl.pallas_call(final_kernel, grid_spec=spec, out_shape=(jax.ShapeDtypeStr...  6.78 us

profile of v2, /device:TPU:74, one launch (start us, length us, event | category | flops | bytes accessed | tf_op | source)
XLA Modules:
  0.0 181.8 jit_solution(17238846938835814374)
XLA Ops:
  0.6 0.6 pad_add_fusion.place
  1.2 0.7 dynamic-slice_convert_fusion
  1.9 0.6 bitcast_add_fusion.shift
  2.6 172.4 %shard_map.50 = (f32[768,768]{1,0:T(8,128)}, f32[768,768]{1,0:T(8,128)}, f32[768,256]{1,0:T(8,128)}) custom-call(f32[1,1536,768]{2,1,0:T(8,128)} %own.1, f32[1,768]{1,0:T(1,128)} %bitcast_add_fusion.shift, f32[1,1536,768]{2,1,0:T(8,128)} %own.1, s32[2,2]{1,0:T(2,128)} %piv.3), custom_call_target="tpu_custom_call" | custom-call | tf_op jit(solution)/shard_map/pallas_call | solution.py:688
  175.0 6.8 %shard_map.51 = (f32[1,1,768,768]{3,2,1,0:T(8,128)}, f32[1,1,768,256]{3,2,1,0:T(8,128)}) custom-call(s32[3]{0:T(128)} %pad_add_fusion.place, s32[2,2]{1,0:T(2,128)} %piv.3, f32[1,1536,768]{2,1,0:T(8,128)} %own.1, f32[768,768]{1,0:T(8,128)} %get-tuple-element.5.raw, f32[768,768]{1,0:T(8,128)} %get-tuple-element.6.corr, f32[768,256]{1,0:T(8,128)} %get-tuple-element.7.low, ...), custom_call_target="tpu_custom_call" | custom-call | tf_op jit(solution)/shard_map/pallas_call | solution.py:767

commit v3 on v2

--- a/solution.py
+++ b/solution.py
@@ -104,9 +104,9 @@
 
 
 def main_kernel(
-    a_ref, shift, prior, piv,
-    raw, corr, low_out,
-    x_buf, r_buf, p0c_buf, n_buf, cand, pcand, cm, pm, rs, y, hpre, p2, p2sum, p3, pv, gr, gsum, gp, g, u, mparts, pparts,
+    a_ref, shift, piv,
+    schur, lower,
+    raw,     x_buf, r_buf, p0c_buf, n_buf, cand, pcand, cm, pm, rs1, rs2, acc, y, hpre, p2, p2sum, p3, pv, gr, gsum, gp, g, u, mparts, pparts,
     sem_p1, sem_c1, sem_h1, s_p2, r_p2, s_p3, r_p3, s_p4, r_p4, s_p5, r_p5,
     s_g1, r_g1, s_g2, r_g2, s_g3, r_g3, s_g4, r_g4,
     s_rs, r_rs, s_h, r_h, s_agr, s_agl, r_ag, s_ahr, s_ahl, r_ah,
@@ -174,9 +174,19 @@
     def p2_copy(o, cc, slot):
         return copy(pm.at[span(32 * cc, 32), :], p2.at[slot], s_p2.at[o - 1], r_p2.at[slot], at(z, cc))
 
-    def rs_copy(o, q, slot):
+    def rs_first(way, layer):
+        q = (layer + 2) % 4
+        k = (1 - way) // 2
         return copy(
-            cm.at[pl.ds(0, 2), span(64 * q, 64), :], rs.at[slot], s_rs.at[o - 1], r_rs.at[slot], at(2 * q + d, c)
+            cm.at[pl.ds(0, 2), span(64 * q + 32 * k, 32), :], rs1.at[k], s_rs.at[k], r_rs.at[k],
+            at(2 * ((layer + way + 4) % 4) + d, c),
+        )
+
+    def rs_second(way, layer):
+        q = (layer + way + 4) % 4
+        k = (1 - way) // 2
+        return copy(
+            acc.at[k], rs2.at[k], s_rs.at[2 + k], r_rs.at[2 + k], at(2 * q + d, c)
         )
 
     def h_copy(q):
@@ -213,8 +223,8 @@
 
     def raw_copy(k):
         return copy(
-            prior.at[0, span((1 - d) * 768 + 256 * k, 256), :],
-            raw.at[pl.ds(256 * k, 256), :], s_raw.at[k], r_raw.at[k], partner,
+            a_ref.at[0, span((1 - d) * 768 + 128 * k, 128), :],
+            raw.at[pl.ds(128 * k, 128), :], s_raw.at[k], r_raw.at[k], partner,
         )
 
     sends_h = (d == 1) & (r == 0)
@@ -228,6 +238,8 @@
     @pl.when(sends_h)
     def _():
         h_first().start()
+
+    raw_copy(0).start()
 
     @pl.when(s == 1)
     def _():
@@ -260,20 +272,6 @@
         @pl.when((r == d) & (d == 1))
         def _():
             cm[2] = jnp.zeros((TILE, 768), F32)
-
-        @pl.when(c == 0)
-        def _():
-            for o in range(1, 4):
-                g1_copy(o, (z_hi + o) % 4, z_hi).start()
-
-        for o in range(1, 4):
-            rs_copy(o, (z_hi + o) % 4, z_hi).start()
-
-        @pl.when(leads_h)
-        def _():
-            for q in range(1, 4):
-                h_copy(q).start()
-            y[2, 0:64, :] = cm[2, 0:64, :]
 
         total = pm[span(32 * c, 32), :]
         for o in range(1, 16):
@@ -284,18 +282,6 @@
         for o in range(1, 4):
             p3_copy(o, (z_hi + o) % 4, z_hi).start()
 
-        @pl.when(c == 0)
-        def _():
-            total = cm[:, span(64 * z_hi, 64), 0:TILE]
-            for o in range(1, 4):
-                q = (z_hi + o) % 4
-                g1_copy(o, q, q).wait_recv()
-                total = total + gr[q]
-            gsum[...] = total
-            for cc in range(1, 8):
-                g2_copy(cc).start()
-            gp[0, :, span(8 * z_hi, 8), :] = total[:, 0:8]
-
         total = p2sum[span(8 * z_hi, 8), :]
         for o in range(1, 4):
             q = (z_hi + o) % 4
@@ -305,14 +291,19 @@
         for o in range(1, 8):
             p4_copy(o, (z + o) % 8, z_hi).start()
 
-        @pl.when((c > 0) & (c < 8))
-        def _():
-            g2_copy(c).wait_recv()
-
-        @pl.when(c < 8)
-        def _():
-            for o in range(1, 8):
-                g3_copy(o, (z + o) % 8, z_hi).start()
+        @pl.when(c == 0)
+        def _():
+            for o in range(1, 4):
+                g1_copy(o, (z_hi + o) % 4, z_hi).start()
+
+        for way in (1, -1):
+            rs_first(way, z_hi).start()
+
+        @pl.when(leads_h)
+        def _():
+            for q in range(1, 4):
+                h_copy(q).start()
+            y[2, 0:64, :] = cm[2, 0:64, :]
 
         for o in range(1, 4):
             q = (z_hi + o) % 4
@@ -325,6 +316,15 @@
 
     for o in range(1, 16):
         p5_copy(o, (c + o) % 16, c).start()
+
+    @pl.when(own)
+    def _():
+        for way in (1, -1):
+            k = (1 - way) // 2
+            rs_first(way, z_hi).wait_recv()
+            acc[k] = cm[0:2, span(64 * ((z_hi + way + 4) % 4), 64), :]
+            acc[k, :, 32 * k : 32 * k + 32, :] = acc[k, :, 32 * k : 32 * k + 32, :] + rs1[k]
+            rs_second(way, z_hi).start()
 
     def order(e, k):
         delta = jnp.where(
@@ -375,23 +375,6 @@
             @pl.when(own)
             def _():
                 arrive(3)
-
-    @pl.when(own)
-    def _():
-        rows = span(64 * z_hi, 64)
-        total = cm[0:2, rows, :]
-        for o in range(1, 4):
-            q = (z_hi + o) % 4
-            rs_copy(o, q, q).wait_recv()
-            total = total + rs[q]
-        y[0:2, rows, :] = total
-
-        @pl.when((d == 0) & (r != 0))
-        def _():
-            h_copy(z_hi).wait_recv()
-
-        Ring(0, 1).both("start")
-        Ring(0, -1).both("start")
 
     k_own = 2 * r + d
     k_sib = 2 * (r + 1 - 2 * s) + d
@@ -489,42 +472,92 @@
     for o in range(1, 16):
         p5_copy(o, (c + o) % 16, c).wait_send()
 
-    @pl.when(own & (c < 8))
-    def _():
-        for o in range(1, 4):
-            q = (z_hi + o) % 4
-            g3_copy(o, z, q).wait_recv()
-
-    @pl.when(other & (c < 8))
-    def _():
-        for q in range(4):
-            g3_copy(1, z, q).wait_recv()
-
-    push_g4()
-
     @pl.when(own)
     def _():
         for o in range(1, 8):
             p4_copy(o, (z + o) % 8, z_hi).wait_send()
 
+    def end_reduce():
+        @pl.when(own)
+        def _():
+            rows = span(64 * z_hi, 64)
+            total = cm[0:2, rows, :]
+            for way in (1, -1):
+                rs_second(way, z_hi).wait_recv()
+                total = total + rs2[(1 - way) // 2]
+            y[0:2, rows, :] = total
+
+            @pl.when((d == 0) & (r != 0))
+            def _():
+                h_copy(z_hi).wait_recv()
+
+            Ring(0, 1).both("start")
+            Ring(0, -1).both("start")
+
+    @pl.when(own)
+    def _():
+        @pl.when(c == 0)
+        def _():
+            total = cm[:, span(64 * z_hi, 64), 0:TILE]
+            for o in range(1, 4):
+                q = (z_hi + o) % 4
+                g1_copy(o, q, q).wait_recv()
+                total = total + gr[q]
+            gsum[...] = total
+            for cc in range(1, 8):
+                g2_copy(cc).start()
+            gp[0, :, span(8 * z_hi, 8), :] = total[:, 0:8]
+
+    def between(p, i):
+        @pl.when((p == 0) & (i == 2) & own)
+        def _():
+            @pl.when((c > 0) & (c < 8))
+            def _():
+                g2_copy(c).wait_recv()
+
+            @pl.when(c < 8)
+            def _():
+                for o in range(1, 8):
+                    g3_copy(o, (z + o) % 8, z_hi).start()
+
+        x_slot(5 * (p - 2) + i)
+
     def outer(p, carry):
-        sweep_step(pv, p, lambda i: x_slot(5 * (p - 1) + i))
-        x_slot(5 * (p - 1) + 4)
-        for k in range(4):
-            @pl.when(p == k)
+        sweep_step(pv, p, lambda i: between(p, i))
+        x_slot(5 * (p - 2) + 4)
+
+        @pl.when(p == 0)
+        def _():
+            end_reduce()
+
+        for k in range(3):
+            @pl.when(p == k + 1)
             def _():
                 stage(k)
-        to_root(p)
-
-        @pl.when(p == 2)
-        def _():
-            raw_copy(0).start()
+
+        @pl.when(p >= 1)
+        def _():
+            to_root(p - 1)
+
+        @pl.when(p == 1)
+        def _():
+            @pl.when(own & (c < 8))
+            def _():
+                for o in range(1, 4):
+                    q = (z_hi + o) % 4
+                    g3_copy(o, z, q).wait_recv()
+
+            @pl.when(other & (c < 8))
+            def _():
+                for q in range(4):
+                    g3_copy(1, z, q).wait_recv()
+
+            push_g4()
 
         return carry
 
     lax.fori_loop(0, 4, outer, 0)
-    raw_copy(1).start()
-    raw_copy(2).start()
+    x_slot(10)
 
     for o in range(1, 16):
         cc = (c + o) % 16
@@ -538,7 +571,7 @@
             for cc in range(8):
                 g[k, 64 * q + 8 * cc : 64 * q + 8 * cc + 8, :] = gp[cc, k, 8 * q : 8 * q + 8, :]
 
-    x_slot(15)
+    x_slot(11)
     gq = g[0:2].reshape(512, TILE)
     us = -dot6(pv[...], gq, ROW_BY_COL)
     u[s] = us
@@ -552,7 +585,12 @@
 
     swap(1, mparts, s).start()
     swap(0, u, s).start()
-    x_slot(16)
+    stage(3)
+    for k in range(1, 6):
+        raw_copy(k).start()
+    to_root(3)
+    x_slot(12)
+    x_slot(13)
 
     t0, t1 = piv[s, 0], piv[s, 1]
 
@@ -565,7 +603,7 @@
         r_buf[2 * s, :, cols] = rk[:TILE]
         r_buf[2 * s + 1, :, cols] = rk[TILE:]
         pparts[s, :, cols] = y[2, :, cols] - dot6(g[0:2].reshape(512, TILE), rk, COL_BY_COL)
-        x_slot(17 + k)
+        x_slot(14 + k)
         return carry
 
     lax.fori_loop(0, 3, r_step, 0)
@@ -577,27 +615,38 @@
 
     def outer_lead(p, carry):
         def two_slots(i):
-            k = 4 * p + i
-            first, last = (7 * k) // 4, (7 * (k + 1)) // 4
-            x_slot(20 + first)
-            x_slot(jnp.where(last - first == 2, 21 + first, -1))
+            x_slot(17 + 8 * p + 2 * i)
+            x_slot(18 + 8 * p + 2 * i)
 
         sweep_step(n_buf, p, two_slots)
         return carry
 
     lax.fori_loop(0, 2, outer_lead, 0)
+    x_slot(33)
     swap(0, u, 1 - s).wait_recv()
 
     swap_r(1 - s).wait_recv()
     swap(3, pparts, 1 - s).wait_recv()
     p0c_buf[...] = pparts[0] + pparts[1]
+
+    for k in range(6):
+        raw_copy(k).wait()
+
+    def zeroed(block, ids, e):
+        ta, tb = piv[e, 0], piv[e, 1]
+        block = block + jnp.where(ids == col_ids, shift[...], 0.0)
+        row_tile, col_tile = ids // TILE, col_ids // TILE
+        hit = (row_tile == ta) | (row_tile == tb) | (col_tile == ta) | (col_tile == tb)
+        return jnp.where(hit, 0.0, block)
 
     def last_step(k, carry):
         cols = pl.ds(pl.multiple_of(k * 256, 256), 256)
         rows = span(k * 256, 256)
         first = k_own * 768 + k * 256
         lead = x_buf[4, :, cols]
-        total = jnp.zeros((TILE, 768), F32)
+        ids = first + iota((TILE, 768), 0)
+        mine = a_ref[0, span(d * 768 + k * 256, 256), :]
+        total = zeroed(mine, ids, d) + zeroed(raw[rows, :], ids, 1 - d)
         for e in range(2):
             ta, tb = piv[e, 0], piv[e, 1]
             xa = modified(x_buf[2 * e, :, cols], ta, tb, first)
@@ -606,9 +655,9 @@
             lead = lead - dot6(u[e], x, COL_BY_COL)
             total = total - dot3(x, r_buf[2 * e : 2 * e + 2].reshape(512, 768), COL_BY_COL)
         low = -dot6(lead, n_buf[...], COL_BY_COL)
-        low_out[rows, :] = low
-        keep = (first + iota((TILE, 768), 0) < TILE) | (col_ids < TILE)
-        corr[rows, :] = total - jnp.where(keep, 0.0, dot3(low, p0c_buf[...], ROW_BY_COL))
+        lower[0, 0, rows, :] = low
+        keep = (ids < TILE) | (col_ids < TILE)
+        schur[0, 0, rows, :] = total - jnp.where(keep, 0.0, dot3(low, p0c_buf[...], ROW_BY_COL))
         return carry
 
     lax.fori_loop(0, 3, last_step, 0)
@@ -629,8 +678,10 @@
     def _():
         for o in range(1, 16):
             p2_copy(o, (c + o) % 16, c).wait_send()
+        for way in (1, -1):
+            rs_first(way, z_hi).wait_send()
+            rs_second(way, z_hi).wait_send()
         for o in range(1, 4):
-            rs_copy(o, (z_hi + o) % 4, z_hi).wait_send()
             p3_copy(o, (z_hi + o) % 4, z_hi).wait_send()
 
         @pl.when(leads_h)
@@ -678,8 +729,6 @@
     swap(1, mparts, s).wait_send()
     swap_r(s).wait_send()
     swap(3, pparts, s).wait_send()
-    for k in range(3):
-        raw_copy(k).wait()
 
 
 def run_main(prior, shift, pivots):
@@ -688,13 +737,13 @@
     return pl.pallas_call(
         main_kernel,
         out_shape=(
-            jax.ShapeDtypeStruct((768, 768), F32),
-            jax.ShapeDtypeStruct((768, 768), F32),
-            jax.ShapeDtypeStruct((768, 256), F32),
+            jax.ShapeDtypeStruct((1, 1, 768, 768), F32),
+            jax.ShapeDtypeStruct((1, 1, 768, TILE), F32),
         ),
-        in_specs=[vmem, vmem, pl.BlockSpec(memory_space=pl.ANY), pl.BlockSpec(memory_space=pltpu.SMEM)],
-        out_specs=(pl.BlockSpec(memory_space=pl.ANY), vmem, vmem),
+        in_specs=[vmem, vmem, pl.BlockSpec(memory_space=pltpu.SMEM)],
+        out_specs=(vmem, vmem),
         scratch_shapes=[
+            pltpu.VMEM((768, 768), F32),
             pltpu.VMEM((5, 256, 768), F32),
             pltpu.VMEM((4, 256, 768), F32),
             pltpu.VMEM((256, 768), F32),
@@ -703,7 +752,9 @@
             pltpu.VMEM((512, 512), F32),
             pltpu.VMEM((3, 256, 768), F32),
             pltpu.VMEM((512, 512), F32),
-            pltpu.VMEM((4, 2, 64, 768), F32),
+            pltpu.VMEM((2, 2, 32, 768), F32),
+            pltpu.VMEM((2, 2, 64, 768), F32),
+            pltpu.VMEM((2, 2, 64, 768), F32),
             pltpu.VMEM((3, 256, 768), F32),
             pltpu.VMEM((256, 768), F32),
             pltpu.VMEM((16, 32, 512), F32),
@@ -720,59 +771,16 @@
             dma((2,)), dma((2,)), dma((2,)),
             dma((15,)), dma((16,)), dma((3,)), dma((4,)), dma((7,)), dma((4,)), dma((15,)), dma((16,)),
             dma((3,)), dma((4,)), dma((7,)), dma((1,)), dma((7,)), dma((4,)), dma((15,)), dma((8,)),
-            dma((3,)), dma((4,)), dma((3,)), dma((1,)),
+            dma((4,)), dma((4,)), dma((3,)), dma((1,)),
             dma((4,)), dma((4,)), dma((4,)), dma((4,)), dma((4,)), dma((4,)),
             dma((4,)), dma((4,)), dma((4,)), dma((4,)),
             dma((4, 20)), dma((4, 20)), dma((4, 20)),
-            dma((3,)), dma((3,)), dma((4,)), dma((4,)),
+            dma((6,)), dma((6,)), dma((4,)), dma((4,)),
         ],
         compiler_params=pltpu.CompilerParams(
             collective_id=0, has_side_effects=True, vmem_limit_bytes=56 * 1024 * 1024
         ),
-    )(prior, shift, prior, pivots)
-
-
-def final_kernel(place, piv, own, raw, corr, low, shift, schur, lower):
-    step = pl.program_id(0)
-    rows = place[1] * 768 + step * 256 + iota((256, 768), 0)
-    cols = place[2] * 768 + iota((256, 768), 1)
-    added = jnp.where(rows == cols, shift[...], 0.0)
-    row_tile, col_tile = rows // TILE, cols // TILE
-
-    def zeroed(block, e):
-        a, b = piv[e, 0], piv[e, 1]
-        hit = (row_tile == a) | (row_tile == b) | (col_tile == a) | (col_tile == b)
-        return jnp.where(hit, 0.0, block + added)
-
-    schur[0, 0] = zeroed(own[0], place[0]) + zeroed(raw[...], 1 - place[0]) + corr[...]
-    lower[0, 0] = low[...]
-
-
-def run_final(place, pivots, prior, raw, corr, low, shift):
-    spec = pltpu.PrefetchScalarGridSpec(
-        num_scalar_prefetch=2,
-        grid=(3,),
-        in_specs=[
-            pl.BlockSpec((1, 256, 768), lambda i, p, v: (0, 3 * p[0] + i, 0)),
-            pl.BlockSpec((256, 768), lambda i, p, v: (i, 0)),
-            pl.BlockSpec((256, 768), lambda i, p, v: (i, 0)),
-            pl.BlockSpec((256, 256), lambda i, p, v: (i, 0)),
-            pl.BlockSpec((1, 768), lambda i, p, v: (0, 0)),
-        ],
-        out_specs=(
-            pl.BlockSpec((1, 1, 256, 768), lambda i, p, v: (0, 0, i, 0)),
-            pl.BlockSpec((1, 1, 256, 256), lambda i, p, v: (0, 0, i, 0)),
-        ),
-    )
-    return pl.pallas_call(
-        final_kernel,
-        grid_spec=spec,
-        out_shape=(
-            jax.ShapeDtypeStruct((1, 1, 768, 768), F32),
-            jax.ShapeDtypeStruct((1, 1, 768, 256), F32),
-        ),
-        compiler_params=pltpu.CompilerParams(vmem_limit_bytes=56 * 1024 * 1024),
-    )(place, pivots, prior, raw, corr, low, shift)
+    )(prior, shift, pivots)
 
 
 def shifts(quantum):
@@ -786,11 +794,9 @@
 
 
 def per_device(prior_y, labels, pivots):
-    r, c, d = lax.axis_index("row"), lax.axis_index("col"), lax.axis_index("dir")
-    shift = shifts(lax.dynamic_slice_in_dim(labels, c * 768, 768, 0))[None, :]
-    raw, corr, low = run_main(prior_y, shift, pivots)
-    place = jnp.stack([d, 2 * r + d, c]).astype(jnp.int32)
-    return run_final(place, pivots, prior_y, raw, corr, low, shift)
+    first = lax.axis_index("col") * 768
+    shift = shifts(lax.dynamic_slice_in_dim(labels, first, 768, 0))[None, :]
+    return run_main(prior_y, shift, pivots)
 
 
 def solution(mesh):

time: 185 us -> 177 us (0.957); the launches traced: 182 us -> 177 us
  Pallas kernels: 179 us -> 171 us
  local copies, waits for them, and re-layouts: 0 us -> 4.18 us
    pallas_call x2 -> x1, Pallas kernels: 179 us -> 171 us  [run_main(): pl.pallas_call(main_kernel, out_shape=(jax.ShapeDtypeStruct((1, 1, 768, 7...]
    unnamed x0 -> x4, local copies, waits for them, and re-layouts: none -> 4.18 us
where the time goes in v3:
time: 177 us
  Pallas kernels  171 us (97%)
  local copies, waits for them, and re-layouts  4.18 us (2%)
    pallas_call x1, Pallas kernels, run_main(): pl.pallas_call(main_kernel, out_shape=(jax.ShapeDtypeStruct((1, 1, 768, 7...  171 us
    unnamed x4, local copies, waits for them, and re-layouts  4.18 us

profile of v3, /device:TPU:74, one launch (start us, length us, event | category | flops | bytes accessed | tf_op | source)
XLA Modules:
  0.0 177.2 jit_solution(11940916765106147780)
XLA Ops:
  0.6 0.7 dynamic-slice_convert_fusion
  1.3 0.6 bitcast_add_fusion.shift
  1.9 171.0 %shard_map.50 = (f32[1,1,768,768]{3,2,1,0:T(8,128)}, f32[1,1,768,256]{3,2,1,0:T(8,128)}) custom-call(f32[1,1536,768]{2,1,0:T(8,128)} %a_ref.1, f32[1,768]{1,0:T(1,128)} %bitcast_add_fusion.shift, s32[2,2]{1,0:T(2,128)} %piv.1), custom_call_target="tpu_custom_call" | custom-call | tf_op jit(solution)/shard_map/pallas_call | solution.py:737
  173.0 0.0 copy-start
  173.0 3.3 %copy.7 = f32[1,1,768,768]{3,2,1,0:T(8,128)} copy(f32[1,1,768,768]{3,2,1,0:T(8,128)} %get-tuple-element.4) | data formatting | bytes 4718592
  176.3 0.0 copy-done
  176.3 0.9 copy.8
Async XLA Ops:
  173.0 3.3 %copy-start = (f32[1,1,768,256]{3,2,1,0:T(8,128)S(1)}, f32[1,1,768,256]{3,2,1,0:T(8,128)}, u32[]{:S(2)}) copy-start(f32[1,1,768,256]{3,2,1,0:T(8,128)} %get-tuple-element.5) | copy-start | bytes 2359300

commit v4 on v3

--- a/solution.py
+++ b/solution.py
@@ -239,8 +239,6 @@
     def _():
         h_first().start()
 
-    raw_copy(0).start()
-
     @pl.when(s == 1)
     def _():
         y[2] = jnp.zeros((TILE, 768), F32)
@@ -426,7 +424,7 @@
             to_x = (dy >= 1) & (dx < 3)
             to_y = ((dx == 0) & (dy < 3)) | ((dx >= 1) & (dy == 3))
             depth = depth + jnp.where((dy == 0) & (dx >= 1), 4, 0)
-        p = slot - 2 * depth
+        p = slot - 3 * depth
         valid = (p >= 0) & (p < 20)
         p = jnp.where(valid, p, 0)
         tile = p % 5
@@ -586,7 +584,7 @@
     swap(1, mparts, s).start()
     swap(0, u, s).start()
     stage(3)
-    for k in range(1, 6):
+    for k in range(6):
         raw_copy(k).start()
     to_root(3)
     x_slot(12)
@@ -614,15 +612,14 @@
     n_buf[...] = mparts[0] + mparts[1]
 
     def outer_lead(p, carry):
-        def two_slots(i):
-            x_slot(17 + 8 * p + 2 * i)
-            x_slot(18 + 8 * p + 2 * i)
-
-        sweep_step(n_buf, p, two_slots)
+        def three_slots(i):
+            for k in range(3):
+                x_slot(17 + 12 * p + 3 * i + k)
+
+        sweep_step(n_buf, p, three_slots)
         return carry
 
     lax.fori_loop(0, 2, outer_lead, 0)
-    x_slot(33)
     swap(0, u, 1 - s).wait_recv()
 
     swap_r(1 - s).wait_recv()
@@ -724,7 +721,7 @@
         x_end(slot)
         return carry
 
-    lax.fori_loop(0, 34, x_last, 0)
+    lax.fori_loop(0, 41, x_last, 0)
     swap(0, u, s).wait_send()
     swap(1, mparts, s).wait_send()
     swap_r(s).wait_send()

time: 177 us -> 177 us (level); the launches traced: 177 us -> 175 us
  Pallas kernels: 171 us -> 169 us
    pallas_call x1, Pallas kernels: 171 us -> 169 us  [run_main(): pl.pallas_call(main_kernel, out_shape=(jax.ShapeDtypeStruct((1, 1, 768, 7...]
where the time goes in v4:
time: 177 us; the launch traced here: 175 us
  Pallas kernels  169 us (95%)
  local copies, waits for them, and re-layouts  4.18 us (2%)
    pallas_call x1, Pallas kernels, run_main(): pl.pallas_call(main_kernel, out_shape=(jax.ShapeDtypeStruct((1, 1, 768, 7...  169 us
    unnamed x4, local copies, waits for them, and re-layouts  4.18 us

profile of v4, /device:TPU:74, one launch (start us, length us, event | category | flops | bytes accessed | tf_op | source)
XLA Modules:
  0.0 175.4 jit_solution(12254615911365659575)
XLA Ops:
  0.6 0.7 dynamic-slice_convert_fusion
  1.3 0.6 bitcast_add_fusion.shift
  1.9 169.2 %shard_map.50 = (f32[1,1,768,768]{3,2,1,0:T(8,128)}, f32[1,1,768,256]{3,2,1,0:T(8,128)}) custom-call(f32[1,1536,768]{2,1,0:T(8,128)} %a_ref.1, f32[1,768]{1,0:T(1,128)} %bitcast_add_fusion.shift, s32[2,2]{1,0:T(2,128)} %piv.1), custom_call_target="tpu_custom_call" | custom-call | tf_op jit(solution)/shard_map/pallas_call | solution.py:734
  171.2 0.0 copy-start
  171.2 3.3 %copy.7 = f32[1,1,768,768]{3,2,1,0:T(8,128)} copy(f32[1,1,768,768]{3,2,1,0:T(8,128)} %get-tuple-element.4) | data formatting | bytes 4718592
  174.5 0.0 copy-done
  174.5 0.9 copy.8
Async XLA Ops:
  171.2 3.3 %copy-start = (f32[1,1,768,256]{3,2,1,0:T(8,128)S(1)}, f32[1,1,768,256]{3,2,1,0:T(8,128)}, u32[]{:S(2)}) copy-start(f32[1,1,768,256]{3,2,1,0:T(8,128)} %get-tuple-element.5) | copy-start | bytes 2359300
